TPU v7x, 128 devices: a whole 4x4x4 slice. The times are simulated.
128 devices in a mesh: sub: 16 (over y, x), blk: 8 (over z, core).
Axes of the slice: x: 4, y: 4, z: 4, core: 2. Of those that a mesh axis runs over, the one named last changes fastest.
Arguments:
- f_local: float32 [256, 16, 1024], P(('sub', 'blk')), may hold values from -6 to 6
- schur: float32 [256, 1024, 1024], P(('sub', 'blk')), as said below
- precond: float32 [256, 1024, 1024], P(('sub', 'blk')), as said below
- modes: float32 [256, 6, 1024], P(('sub', 'blk')), may hold values from -0.1875 to 0.1875
- coarse_inv: float32 [1536, 1536], P(('sub', 'blk')), as said below
- nbr_sub: int32 [256, 8], P(('sub', 'blk')), may hold values from -1 to 255, as said below
- nbr_blk: int32 [256, 8], P(('sub', 'blk')), may hold values from -1 to 7, as said below
Outputs:
- lambda_sol: float32 [256, 16, 1024], P(('sub', 'blk'))
- proj_residual: float32 [256, 16, 1024], P(('sub', 'blk'))
Inputs may be any that keep to these rules, and one draw needn't show every extreme that they name: `nbr_sub`: sharing is mutual: if block j of subdomain s names block j2 of subdomain s2, that block names block j of s. The partner lies on the device next along sub or next along blk (either way, cyclic), with subdomains numbered in device order; each such pair of devices shares 1 to 4 blocks, and some pair shares exactly 4. `nbr_blk`: -1 exactly where nbr_sub is -1. `schur`: each subdomain's matrix is symmetric positive definite. `precond`: each subdomain's matrix is symmetric positive definite. `coarse_inv`: symmetric positive definite.
All inputs are finite; a program needn't handle non-finite values.
Results may differ from a plain program's by a relative error of at most 0.00017.
Values sent between devices are 32-bit elements; how exact they have to be, the bound alone decides.
A program may use at most 64 MiB of HBM per device.

v0:
```python
import jax
import jax.numpy as jnp
from jax import lax
from jax.sharding import PartitionSpec as P

ITERS = 2


def with_halo(cells, sides, width):
    for axis, dim in sides:
        count = lax.axis_size(axis)
        head = lax.slice_in_dim(cells, 0, width, axis=dim)
        tail = lax.slice_in_dim(cells, cells.shape[dim] - width, cells.shape[dim], axis=dim)
        cells = jnp.concatenate(
            [
                lax.ppermute(tail, axis, [(i, (i + 1) % count) for i in range(count)]),
                cells,
                lax.ppermute(head, axis, [((i + 1) % count, i) for i in range(count)]),
            ],
            axis=dim,
        )
    return cells


def neighbour_layout(nbr_sub, nbr_blk):
    num_slots = nbr_sub.shape[0]
    size_sub = lax.axis_size("sub")
    size_blk = lax.axis_size("blk")
    here_sub = lax.axis_index("sub")
    here_blk = lax.axis_index("blk")
    paired = nbr_sub >= 0
    partner_id = jnp.where(paired, nbr_sub, 0)
    device = partner_id // num_slots
    step_sub = (device // size_blk - here_sub + 1 + size_sub) % size_sub - 1
    step_blk = (device % size_blk - here_blk + 1 + size_blk) % size_blk - 1
    local_slot = partner_id % num_slots
    partner_col = jnp.where(paired, nbr_blk, 0)
    return (paired, step_sub, step_blk, local_slot, partner_col)


def pick_partner(framed, layout_info, out_shape):
    paired, step_sub, step_blk, local_slot, partner_col = layout_info
    num_slots, num_cases, num_width = out_shape
    num_blocks = paired.shape[1]
    framed = framed.reshape(9 * num_slots, num_cases, num_blocks, num_width // num_blocks)
    source_rows = ((step_sub + 1) * 3 + step_blk + 1) * num_slots + local_slot
    picked = framed[source_rows, :, partner_col, :]
    picked = jnp.transpose(picked, (0, 2, 1, 3)) * paired.astype(jnp.float32)[:, None, :, None]
    return picked.reshape(out_shape)


def partner_framed(values, layout_info):
    framed = with_halo(values[None, None], (("sub", 0), ("blk", 1)), 1)
    return pick_partner(framed, layout_info, values.shape)


def assemble(values, layout_info):
    return values - partner_framed(values, layout_info)


def weighted_dot(left, right, weights):
    num_slots, num_cases, num_width = left.shape
    num_blocks = weights.shape[1]
    per_block = jnp.sum(
        (left * right).reshape(num_slots, num_cases, num_blocks, num_width // num_blocks), axis=3
    )
    return jnp.sum(per_block * weights[:, None, :], axis=(0, 2))


def coarse_factors(moments, coarse_rows):
    every_moment = lax.all_gather(moments, ("sub", "blk"), axis=1, tiled=True)
    return jnp.einsum("kn,cn->ck", coarse_rows, every_moment, precision=lax.Precision.HIGHEST)


def project(values, modes, coarse_rows, layout_info):
    num_slots, num_cases, num_width = values.shape
    num_modes = modes.shape[1]
    moments = jnp.einsum("smn,scn->csm", modes, values, precision=lax.Precision.HIGHEST).reshape(
        num_cases, -1
    )
    factors = coarse_factors(moments, coarse_rows)
    spread = jnp.einsum(
        "smn,csm->scn",
        modes,
        factors.reshape(num_cases, num_slots, num_modes),
        precision=lax.Precision.HIGHEST,
    )
    return values - assemble(spread, layout_info)


def apply_local(matrices, values):
    return jnp.einsum("sij,scj->sci", matrices, values, precision=lax.Precision.HIGHEST)


def per_device(f_local, schur, precond, modes, coarse_inv, nbr_sub, nbr_blk):
    layout_info = neighbour_layout(nbr_sub, nbr_blk)
    weights = jnp.where(layout_info[0], 0.5, 1.0).astype(jnp.float32)
    num_cases = f_local.shape[1]
    residual = assemble(f_local, layout_info)
    proj_residual = project(residual, modes, coarse_inv, layout_info)
    lambda_sol = jnp.zeros_like(f_local)
    direction = jnp.zeros_like(f_local)
    rho_before = jnp.ones((num_cases,), jnp.float32)
    for iteration in range(ITERS):
        precond_out = assemble(apply_local(precond, proj_residual), layout_info)
        search = project(precond_out, modes, coarse_inv, layout_info)
        rho_now = lax.psum(weighted_dot(search, residual, weights), ("sub", "blk"))
        if iteration == 0:
            direction = search
        else:
            direction = search + (rho_now / rho_before)[None, :, None] * direction
        image = assemble(apply_local(schur, direction), layout_info)
        sigma_now = lax.psum(weighted_dot(direction, image, weights), ("sub", "blk"))
        step_size = (rho_now / sigma_now)[None, :, None]
        lambda_sol = lambda_sol + step_size * direction
        residual = residual - step_size * image
        proj_residual = project(residual, modes, coarse_inv, layout_info)
        rho_before = rho_now
    return (lambda_sol, proj_residual)


def solution(mesh):
    return jax.shard_map(
        per_device,
        mesh=mesh,
        in_specs=(
            P(("sub", "blk"), None, None),
            P(("sub", "blk"), None, None),
            P(("sub", "blk"), None, None),
            P(("sub", "blk"), None, None),
            P(("sub", "blk"), None),
            P(("sub", "blk"), None),
            P(("sub", "blk"), None),
        ),
        out_specs=(P(("sub", "blk"), None, None), P(("sub", "blk"), None, None)),
        check_vma=False,
    )
```

profile of v0, /device:TPU:1, one launch (start us, length us, event | category | flops | bytes accessed | tf_op | source)
XLA Modules:
  0.0 613.8 jit_solution(2165139081438343930)
XLA Ops:
  0.6 5.8 collective-permute-start.1
  26.7 37.1 %all-gather = f32[128,12,16]{2,1,0:T(8,128)S(1)} all-gather(f32[1,12,16]{2,1,0:T(8,128)S(1)} %bitcast.341), channel_id=1, replica_groups=mesh['sub'=16,'blk'=8] {'sub','blk'}, dimensions={0}, use_global_device_ids=true | all-gather | bytes 99072 | tf_op jit(solution)/shard_map/all_gather | solution.py:71
  70.0 5.2 collective-permute-done.4
  76.9 5.8 collective-permute-done.7
  83.9 9.3 %fusion.8 = f32[2,16,1024]{2,1,0:T(8,128)S(1)} fusion(f32[2,1024,1024]{2,1,0:T(8,128)} %param.9, f32[2,16,1024]{2,1,0:T(8,128)S(1)} %bitcast_subtract_fusion.9, f32[2,16,1024]{2,1,0:T(8,128)S(1)} %fusion.23, f32[2,8,16,128]{3,2,1,0:T(8,128)S(1)} %bitcast.327, f32[2,8]{1,0:T(2,128)S(1)} %fusion.40), kind=kOutput, calls=%fused_computation.55 | convolution fusion | flops 402751488 | bytes 8912960 | tf_op jit(solution)/shard_map/sij,scj->sci/dot_general | solution.py:92
  104.0 5.3 collective-permute-done.11
  110.8 37.2 %all-gather.1 = f32[128,12,16]{2,1,0:T(8,128)S(1)} all-gather(f32[1,12,16]{2,1,0:T(8,128)S(1)} %bitcast.342), channel_id=1, replica_groups=mesh['sub'=16,'blk'=8] {'sub','blk'}, dimensions={0}, use_global_device_ids=true | all-gather | bytes 99072 | tf_op jit(solution)/shard_map/all_gather | solution.py:71
  154.3 5.2 collective-permute-done.12
  161.3 5.8 collective-permute-done.15
  168.3 9.2 %fusion.48 = f32[2,16,1024]{2,1,0:T(8,128)S(1)} fusion(f32[2,16,1024]{2,1,0:T(8,128)S(1)} %get-tuple-element.9, f32[2,1024,1024]{2,1,0:T(8,128)} %param.8), kind=kOutput, calls=%fused_computation.131 | convolution fusion | flops 402653184 | bytes 8650752 | tf_op jit(solution)/shard_map/sij,scj->sci/dot_general | solution.py:92
  188.4 5.2 collective-permute-done.19
  195.3 64.5 %all-reduce = (f32[16]{0:T(128)S(1)}, f32[16]{0:T(128)S(1)}) all-reduce(f32[16]{0:T(128)S(1)} %get-tuple-element.3, f32[16]{0:T(128)S(1)} %get-tuple-element.2), channel_id=1, replica_groups=mesh['sub'=16,'blk'=8] {'sub','blk'}, use_global_device_ids=true, to_apply=%region_2.3 | all-reduce | flops 32 | bytes 256 | tf_op jit(solution)/shard_map/psum | solution.py:107
  260.1 35.2 %all-gather.2 = f32[128,12,16]{2,1,0:T(8,128)S(1)} all-gather(f32[1,12,16]{2,1,0:T(8,128)S(1)} %bitcast.343), channel_id=1, replica_groups=mesh['sub'=16,'blk'=8] {'sub','blk'}, dimensions={0}, use_global_device_ids=true | all-gather | bytes 99072 | tf_op jit(solution)/shard_map/all_gather | solution.py:71
  308.6 5.8 collective-permute-done.23
  315.5 9.3 %fusion.3 = f32[2,16,1024]{2,1,0:T(8,128)S(1)} fusion(f32[2,1024,1024]{2,1,0:T(8,128)} %param.9, f32[2,16,1024]{2,1,0:T(8,128)S(1)} %multiply_subtract_fusion.1, f32[2,16,1024]{2,1,0:T(8,128)S(1)} %fusion.17, f32[2,8,16,128]{3,2,1,0:T(8,128)S(1)} %bitcast.328, f32[2,8]{1,0:T(2,128)S(1)} %fusion.40), kind=kOutput, calls=%fused_computation.47 | convolution fusion | flops 402751488 | bytes 8912960 | tf_op jit(solution)/shard_map/sij,scj->sci/dot_general | solution.py:92
  335.6 5.3 collective-permute-done.27
  342.4 37.5 %all-gather.3 = f32[128,12,16]{2,1,0:T(8,128)S(1)} all-gather(f32[1,12,16]{2,1,0:T(8,128)S(1)} %bitcast.344), channel_id=1, replica_groups=mesh['sub'=16,'blk'=8] {'sub','blk'}, dimensions={0}, use_global_device_ids=true | all-gather | bytes 99072 | tf_op jit(solution)/shard_map/all_gather | solution.py:71
  393.1 5.8 collective-permute-done.31
  400.4 63.6 %psum.30 = f32[16]{0:T(128)S(1)} all-reduce(f32[16]{0:T(128)S(1)} %multiply_reduce_fusion.1), channel_id=1, replica_groups=mesh['sub'=16,'blk'=8] {'sub','blk'}, use_global_device_ids=true, to_apply=%region_8.9 | all-reduce | flops 16 | bytes 128 | tf_op jit(solution)/shard_map/psum | solution.py:107
  464.0 9.4 %fusion.41 = f32[2,16,1024]{2,1,0:T(8,128)S(1)} fusion(f32[2,1024,1024]{2,1,0:T(8,128)} %param.8, f32[2,16,1024]{2,1,0:T(8,128)S(1)} %get-tuple-element.7, f32[2,16,1024]{2,1,0:T(8,128)S(1)} %get-tuple-element.9, f32[16]{0:T(128)S(1)} %div.37), kind=kOutput, calls=%fused_computation.126 | convolution fusion | flops 402718720 | bytes 8781888 | tf_op jit(solution)/shard_map/sij,scj->sci/dot_general | solution.py:92
  485.1 5.4 collective-permute-done.35
  492.0 64.4 %psum.31 = f32[16]{0:T(128)S(1)} all-reduce(f32[16]{0:T(128)S(1)} %multiply_reduce_fusion), channel_id=1, replica_groups=mesh['sub'=16,'blk'=8] {'sub','blk'}, use_global_device_ids=true, to_apply=%region_11.12 | all-reduce | flops 16 | bytes 128 | tf_op jit(solution)/shard_map/psum | solution.py:113
  557.5 35.2 %all-gather.4 = f32[128,12,16]{2,1,0:T(8,128)S(1)} all-gather(f32[1,12,16]{2,1,0:T(8,128)S(1)} %bitcast.345), channel_id=1, replica_groups=mesh['sub'=16,'blk'=8] {'sub','blk'}, dimensions={0}, use_global_device_ids=true | all-gather | bytes 99072 | tf_op jit(solution)/shard_map/all_gather | solution.py:71
  605.9 5.8 collective-permute-done.39
  (181 shorter events, 134.2 us)
Async XLA Ops:
  0.6 8.3 %collective-permute-start.1 = (f32[1,1,2,16,1024]{4,3,2,1,0:T(8,128)}, f32[1,1,2,16,1024]{4,3,2,1,0:T(8,128)S(1)}, u32[]{:S(2)}, u32[]{:S(2)}) collective-permute-start(f32[1,1,2,16,1024]{4,3,2,1,0:T(8,128)} %bitcast.315), channel_id=1, source_target_pairs={{8,0},{16,8},{24,16},{32,24},{40,32},{48,40},{56,48},{64,56},{72,6... | collective-permute-start | bytes 393224 | tf_op jit(solution)/shard_map/ppermute | solution.py:18
  6.5 7.3 %collective-permute-start = (f32[1,1,2,16,1024]{4,3,2,1,0:T(8,128)}, f32[1,1,2,16,1024]{4,3,2,1,0:T(8,128)S(1)}, u32[]{:S(2)}, u32[]{:S(2)}) collective-permute-start(f32[1,1,2,16,1024]{4,3,2,1,0:T(8,128)} %bitcast.316), channel_id=1, source_target_pairs={{0,8},{8,16},{16,24},{24,32},{32,40},{40,48},{48,56},{56,64},{64,7... | collective-permute-start | bytes 393224 | tf_op jit(solution)/shard_map/ppermute | solution.py:16
  14.8 9.4 %collective-permute-start.3 = (f32[3,1,2,16,1024]{4,3,2,1,0:T(8,128)S(1)}, f32[3,1,2,16,1024]{4,3,2,1,0:T(8,128)S(1)}, u32[]{:S(2)}, u32[]{:S(2)}) collective-permute-start(f32[3,1,2,16,1024]{4,3,2,1,0:T(8,128)S(1)} %pad_maximum_fusion.10), channel_id=1, source_target_pairs={{1,0},{2,1},{3,2},{4,3},{5,4},{6,5},{7,6},{0,7},{9,8},{10,9},{11,1... | collective-permute-start | bytes 1179656 | tf_op jit(solution)/shard_map/ppermute | solution.py:18
  16.9 7.3 %collective-permute-start.2 = (f32[3,1,2,16,1024]{4,3,2,1,0:T(8,128)S(1)}, f32[3,1,2,16,1024]{4,3,2,1,0:T(8,128)S(1)}, u32[]{:S(2)}, u32[]{:S(2)}) collective-permute-start(f32[3,1,2,16,1024]{4,3,2,1,0:T(8,128)S(1)} %pad_maximum_fusion.10), channel_id=1, source_target_pairs={{0,1},{1,2},{2,3},{3,4},{4,5},{5,6},{6,7},{7,0},{8,9},{9,10},{10,1... | collective-permute-start | bytes 1179656 | tf_op jit(solution)/shard_map/ppermute | solution.py:16
  67.2 8.0 %collective-permute-start.4 = (f32[1,1,2,16,1024]{4,3,2,1,0:T(8,128)S(1)}, f32[1,1,2,16,1024]{4,3,2,1,0:T(8,128)S(1)}, u32[]{:S(2)}, u32[]{:S(2)}) collective-permute-start(f32[1,1,2,16,1024]{4,3,2,1,0:T(8,128)S(1)} %bitcast.296), channel_id=1, source_target_pairs={{0,8},{8,16},{16,24},{24,32},{32,40},{40,48},{48,56},{56,64},{64,7... | collective-permute-start | bytes 393224 | tf_op jit(solution)/shard_map/ppermute | solution.py:16
  75.2 7.5 %collective-permute-start.7 = (f32[3,1,2,16,1024]{4,3,2,1,0:T(8,128)S(1)}, f32[3,1,2,16,1024]{4,3,2,1,0:T(8,128)S(1)}, u32[]{:S(2)}, u32[]{:S(2)}) collective-permute-start(f32[3,1,2,16,1024]{4,3,2,1,0:T(8,128)S(1)} %pad_maximum_fusion.11), channel_id=1, source_target_pairs={{1,0},{2,1},{3,2},{4,3},{5,4},{6,5},{7,6},{0,7},{9,8},{10,9},{11,1... | collective-permute-start | bytes 1179656 | tf_op jit(solution)/shard_map/ppermute | solution.py:18
  76.5 6.2 %collective-permute-start.6 = (f32[3,1,2,16,1024]{4,3,2,1,0:T(8,128)S(1)}, f32[3,1,2,16,1024]{4,3,2,1,0:T(8,128)S(1)}, u32[]{:S(2)}, u32[]{:S(2)}) collective-permute-start(f32[3,1,2,16,1024]{4,3,2,1,0:T(8,128)S(1)} %pad_maximum_fusion.11), channel_id=1, source_target_pairs={{0,1},{1,2},{2,3},{3,4},{4,5},{5,6},{6,7},{7,0},{8,9},{9,10},{10,1... | collective-permute-start | bytes 1179656 | tf_op jit(solution)/shard_map/ppermute | solution.py:16
  93.5 7.1 %collective-permute-start.8 = (f32[1,1,2,16,1024]{4,3,2,1,0:T(8,128)S(1)}, f32[1,1,2,16,1024]{4,3,2,1,0:T(8,128)S(1)}, u32[]{:S(2)}, u32[]{:S(2)}) collective-permute-start(f32[1,1,2,16,1024]{4,3,2,1,0:T(8,128)S(1)} %bitcast.280), channel_id=1, source_target_pairs={{0,8},{8,16},{16,24},{24,32},{32,40},{40,48},{48,56},{56,64},{64,7... | collective-permute-start | bytes 393224 | tf_op jit(solution)/shard_map/ppermute | solution.py:16
  100.7 8.6 %collective-permute-start.11 = (f32[3,1,2,16,1024]{4,3,2,1,0:T(8,128)S(1)}, f32[3,1,2,16,1024]{4,3,2,1,0:T(8,128)S(1)}, u32[]{:S(2)}, u32[]{:S(2)}) collective-permute-start(f32[3,1,2,16,1024]{4,3,2,1,0:T(8,128)S(1)} %pad_maximum_fusion.12), channel_id=1, source_target_pairs={{1,0},{2,1},{3,2},{4,3},{5,4},{6,5},{7,6},{0,7},{9,8},{10,9},{11,1... | collective-permute-start | bytes 1179656 | tf_op jit(solution)/shard_map/ppermute | solution.py:18
  151.5 7.9 %collective-permute-start.12 = (f32[1,1,2,16,1024]{4,3,2,1,0:T(8,128)S(1)}, f32[1,1,2,16,1024]{4,3,2,1,0:T(8,128)S(1)}, u32[]{:S(2)}, u32[]{:S(2)}) collective-permute-start(f32[1,1,2,16,1024]{4,3,2,1,0:T(8,128)S(1)} %bitcast.304), channel_id=1, source_target_pairs={{0,8},{8,16},{16,24},{24,32},{32,40},{40,48},{48,56},{56,64},{64,7... | collective-permute-start | bytes 393224 | tf_op jit(solution)/shard_map/ppermute | solution.py:16
  159.5 7.5 %collective-permute-start.15 = (f32[3,1,2,16,1024]{4,3,2,1,0:T(8,128)S(1)}, f32[3,1,2,16,1024]{4,3,2,1,0:T(8,128)S(1)}, u32[]{:S(2)}, u32[]{:S(2)}) collective-permute-start(f32[3,1,2,16,1024]{4,3,2,1,0:T(8,128)S(1)} %pad_maximum_fusion.13), channel_id=1, source_target_pairs={{1,0},{2,1},{3,2},{4,3},{5,4},{6,5},{7,6},{0,7},{9,8},{10,9},{11,1... | collective-permute-start | bytes 1179656 | tf_op jit(solution)/shard_map/ppermute | solution.py:18
  177.9 7.1 %collective-permute-start.16 = (f32[1,1,2,16,1024]{4,3,2,1,0:T(8,128)S(1)}, f32[1,1,2,16,1024]{4,3,2,1,0:T(8,128)S(1)}, u32[]{:S(2)}, u32[]{:S(2)}) collective-permute-start(f32[1,1,2,16,1024]{4,3,2,1,0:T(8,128)S(1)} %bitcast.288), channel_id=1, source_target_pairs={{0,8},{8,16},{16,24},{24,32},{32,40},{40,48},{48,56},{56,64},{64,7... | collective-permute-start | bytes 393224 | tf_op jit(solution)/shard_map/ppermute | solution.py:16
  185.0 8.6 %collective-permute-start.19 = (f32[3,1,2,16,1024]{4,3,2,1,0:T(8,128)S(1)}, f32[3,1,2,16,1024]{4,3,2,1,0:T(8,128)S(1)}, u32[]{:S(2)}, u32[]{:S(2)}) collective-permute-start(f32[3,1,2,16,1024]{4,3,2,1,0:T(8,128)S(1)} %pad_maximum_fusion.14), channel_id=1, source_target_pairs={{1,0},{2,1},{3,2},{4,3},{5,4},{6,5},{7,6},{0,7},{9,8},{10,9},{11,1... | collective-permute-start | bytes 1179656 | tf_op jit(solution)/shard_map/ppermute | solution.py:18
  298.8 7.9 %collective-permute-start.20 = (f32[1,1,2,16,1024]{4,3,2,1,0:T(8,128)S(1)}, f32[1,1,2,16,1024]{4,3,2,1,0:T(8,128)S(1)}, u32[]{:S(2)}, u32[]{:S(2)}) collective-permute-start(f32[1,1,2,16,1024]{4,3,2,1,0:T(8,128)S(1)} %bitcast.300), channel_id=1, source_target_pairs={{0,8},{8,16},{16,24},{24,32},{32,40},{40,48},{48,56},{56,64},{64,7... | collective-permute-start | bytes 393224 | tf_op jit(solution)/shard_map/ppermute | solution.py:16
  306.8 7.5 %collective-permute-start.23 = (f32[3,1,2,16,1024]{4,3,2,1,0:T(8,128)S(1)}, f32[3,1,2,16,1024]{4,3,2,1,0:T(8,128)S(1)}, u32[]{:S(2)}, u32[]{:S(2)}) collective-permute-start(f32[3,1,2,16,1024]{4,3,2,1,0:T(8,128)S(1)} %pad_maximum_fusion.15), channel_id=1, source_target_pairs={{1,0},{2,1},{3,2},{4,3},{5,4},{6,5},{7,6},{0,7},{9,8},{10,9},{11,1... | collective-permute-start | bytes 1179656 | tf_op jit(solution)/shard_map/ppermute | solution.py:18
  325.1 7.1 %collective-permute-start.24 = (f32[1,1,2,16,1024]{4,3,2,1,0:T(8,128)S(1)}, f32[1,1,2,16,1024]{4,3,2,1,0:T(8,128)S(1)}, u32[]{:S(2)}, u32[]{:S(2)}) collective-permute-start(f32[1,1,2,16,1024]{4,3,2,1,0:T(8,128)S(1)} %bitcast.284), channel_id=1, source_target_pairs={{0,8},{8,16},{16,24},{24,32},{32,40},{40,48},{48,56},{56,64},{64,7... | collective-permute-start | bytes 393224 | tf_op jit(solution)/shard_map/ppermute | solution.py:16
  332.3 8.6 %collective-permute-start.27 = (f32[3,1,2,16,1024]{4,3,2,1,0:T(8,128)S(1)}, f32[3,1,2,16,1024]{4,3,2,1,0:T(8,128)S(1)}, u32[]{:S(2)}, u32[]{:S(2)}) collective-permute-start(f32[3,1,2,16,1024]{4,3,2,1,0:T(8,128)S(1)} %pad_maximum_fusion.16), channel_id=1, source_target_pairs={{1,0},{2,1},{3,2},{4,3},{5,4},{6,5},{7,6},{0,7},{9,8},{10,9},{11,1... | collective-permute-start | bytes 1179656 | tf_op jit(solution)/shard_map/ppermute | solution.py:18
  383.4 8.0 %collective-permute-start.28 = (f32[1,1,2,16,1024]{4,3,2,1,0:T(8,128)S(1)}, f32[1,1,2,16,1024]{4,3,2,1,0:T(8,128)S(1)}, u32[]{:S(2)}, u32[]{:S(2)}) collective-permute-start(f32[1,1,2,16,1024]{4,3,2,1,0:T(8,128)S(1)} %bitcast.308), channel_id=1, source_target_pairs={{0,8},{8,16},{16,24},{24,32},{32,40},{40,48},{48,56},{56,64},{64,7... | collective-permute-start | bytes 393224 | tf_op jit(solution)/shard_map/ppermute | solution.py:16
  391.4 7.5 %collective-permute-start.31 = (f32[3,1,2,16,1024]{4,3,2,1,0:T(8,128)S(1)}, f32[3,1,2,16,1024]{4,3,2,1,0:T(8,128)S(1)}, u32[]{:S(2)}, u32[]{:S(2)}) collective-permute-start(f32[3,1,2,16,1024]{4,3,2,1,0:T(8,128)S(1)} %pad_maximum_fusion.17), channel_id=1, source_target_pairs={{1,0},{2,1},{3,2},{4,3},{5,4},{6,5},{7,6},{0,7},{9,8},{10,9},{11,1... | collective-permute-start | bytes 1179656 | tf_op jit(solution)/shard_map/ppermute | solution.py:18
  392.7 6.2 %collective-permute-start.30 = (f32[3,1,2,16,1024]{4,3,2,1,0:T(8,128)S(1)}, f32[3,1,2,16,1024]{4,3,2,1,0:T(8,128)S(1)}, u32[]{:S(2)}, u32[]{:S(2)}) collective-permute-start(f32[3,1,2,16,1024]{4,3,2,1,0:T(8,128)S(1)} %pad_maximum_fusion.17), channel_id=1, source_target_pairs={{0,1},{1,2},{2,3},{3,4},{4,5},{5,6},{6,7},{7,0},{8,9},{9,10},{10,1... | collective-permute-start | bytes 1179656 | tf_op jit(solution)/shard_map/ppermute | solution.py:16
  475.8 7.1 %collective-permute-start.32 = (f32[1,1,2,16,1024]{4,3,2,1,0:T(8,128)S(1)}, f32[1,1,2,16,1024]{4,3,2,1,0:T(8,128)S(1)}, u32[]{:S(2)}, u32[]{:S(2)}) collective-permute-start(f32[1,1,2,16,1024]{4,3,2,1,0:T(8,128)S(1)} %bitcast.292), channel_id=1, source_target_pairs={{0,8},{8,16},{16,24},{24,32},{32,40},{40,48},{48,56},{56,64},{64,7... | collective-permute-start | bytes 393224 | tf_op jit(solution)/shard_map/ppermute | solution.py:16
  483.0 7.5 %collective-permute-start.35 = (f32[3,1,2,16,1024]{4,3,2,1,0:T(8,128)S(1)}, f32[3,1,2,16,1024]{4,3,2,1,0:T(8,128)S(1)}, u32[]{:S(2)}, u32[]{:S(2)}) collective-permute-start(f32[3,1,2,16,1024]{4,3,2,1,0:T(8,128)S(1)} %pad_maximum_fusion.18), channel_id=1, source_target_pairs={{1,0},{2,1},{3,2},{4,3},{5,4},{6,5},{7,6},{0,7},{9,8},{10,9},{11,1... | collective-permute-start | bytes 1179656 | tf_op jit(solution)/shard_map/ppermute | solution.py:18
  596.2 8.0 %collective-permute-start.36 = (f32[1,1,2,16,1024]{4,3,2,1,0:T(8,128)S(1)}, f32[1,1,2,16,1024]{4,3,2,1,0:T(8,128)S(1)}, u32[]{:S(2)}, u32[]{:S(2)}) collective-permute-start(f32[1,1,2,16,1024]{4,3,2,1,0:T(8,128)S(1)} %bitcast.312), channel_id=1, source_target_pairs={{0,8},{8,16},{16,24},{24,32},{32,40},{40,48},{48,56},{56,64},{64,7... | collective-permute-start | bytes 393224 | tf_op jit(solution)/shard_map/ppermute | solution.py:16
  604.1 7.5 %collective-permute-start.39 = (f32[3,1,2,16,1024]{4,3,2,1,0:T(8,128)S(1)}, f32[3,1,2,16,1024]{4,3,2,1,0:T(8,128)S(1)}, u32[]{:S(2)}, u32[]{:S(2)}) collective-permute-start(f32[3,1,2,16,1024]{4,3,2,1,0:T(8,128)S(1)} %pad_maximum_fusion.19), channel_id=1, source_target_pairs={{1,0},{2,1},{3,2},{4,3},{5,4},{6,5},{7,6},{0,7},{9,8},{10,9},{11,1... | collective-permute-start | bytes 1179656 | tf_op jit(solution)/shard_map/ppermute | solution.py:18
  (20 other events, 167.1 us)
where the time goes:
time: 623 us; the launch traced here: 614 us
  blocking collectives  375 us (60%)
  waiting for transfers between devices  126 us (20%)
  starting transfers between devices  49.6 us (8%)
  matrix products  43 us (7%)
  local copies, waits for them, and re-layouts  11.1 us (2%)
  other arithmetic  7.4 us (1%)
    all_gather x5, blocking collectives, coarse_factors(): every_moment = lax.all_gather(moments, ('sub', 'blk'), axis=1, tiled=True)  182 us
    psum x2, blocking collectives, per_device(): rho_now = lax.psum(weighted_dot(search, residual, weights), ('sub', 'blk'))  128 us
    ppermute x20, waiting for transfers between devices, with_halo(): lax.ppermute(head, axis, [((i + 1) % count, i) for i in range(count)])  79.6 us
    psum x1, blocking collectives, per_device(): lax.psum(weighted_dot(direction, image, weights), ('sub', 'blk'))  64.4 us
    ppermute x20, waiting for transfers between devices, with_halo(): lax.ppermute(tail, axis, [(i, (i + 1) % count) for i in range(count)])  46.8 us
    ppermute x20, starting transfers between devices, with_halo(): lax.ppermute(head, axis, [((i + 1) % count, i) for i in range(count)])  42.3 us
    dot_general x4, matrix products, apply_local(): jnp.einsum('sij,scj->sci', matrices, values, precision=lax.Precision.HIGH...  37.1 us
  transfers between devices with their start and end apart: 40, of which 30 were waited for; matrix products, arithmetic and copies ran while one was open for 0% of the time, Pallas kernels for 0%

commit v1 on v0

v1 whole, which is shorter than its diff:
```python
import jax
import jax.numpy as jnp
from jax import lax
from jax.experimental import pallas as pl
from jax.experimental.pallas import tpu as pltpu
from jax.sharding import PartitionSpec as P

ITERS = 2
GATHERS = 1 + 2 * ITERS
SWAPS = 2 * ITERS
NSUB_AX, NBLK_AX = 16, 8
ROWS = 80
MESH = pl.DeviceIdType.MESH
F32, BF16 = jnp.float32, jnp.bfloat16


def split(x):
    hi = x.astype(BF16)
    return hi, (x - hi.astype(F32)).astype(BF16)


def dot(a, b):
    return jnp.dot(a, b, preferred_element_type=F32)


def dot_t(a, b):
    return lax.dot_general(a, b, (((1,), (1,)), ((), ())), preferred_element_type=F32)


def product3(x, hi, lo, mul=dot):
    rows = x.shape[0]
    xh, xl = split(x)
    both = mul(jnp.concatenate([xh, xl], axis=0), hi)
    return both[:rows] + both[rows:] + mul(xh, lo)


def kernel(
    nsub_ref, nblk_ref, f_hbm, schur_hbm, precond_hbm, modes_hbm, coarse_hbm,
    lam_ref, out_ref,
    fv, mv, stage, khi, klo, shi, slo,
    group, key, source, pick,
    fsend, frecv, mown, msend, mrecv, crows, chi, clo,
    aghi, aglo, kaghi, kaglo, saghi, saglo, ghi, glo,
    wsend, wrecv0, wrecv1, wrecv2, wrecv3, wblk, gath,
    res, kres, zvec, szvec, dirv, qvec, fres,
    hsem, ssem0, rsem0, ssemx, rsemx, ssemg, rsemg,
):
    i, j = lax.axis_index("sub"), lax.axis_index("blk")
    me = i * NBLK_AX + j
    wrecv = (wrecv0, wrecv1, wrecv2, wrecv3)
    yy, xx, zz, cc = i // 4, lax.rem(i, 4), j // 2, lax.rem(j, 2)
    around = [
        (lax.rem(i + 1, NSUB_AX), j),
        (lax.rem(i + NSUB_AX - 1, NSUB_AX), j),
        (i, lax.rem(j + 1, NBLK_AX)),
        (i, lax.rem(j + NBLK_AX - 1, NBLK_AX)),
    ]

    def far(q):
        return 2 + (q * (q + 1)) // 2

    def other(t):
        y = lax.rem(yy + far(t // 32), 4)
        x = lax.rem(xx + far(lax.rem(t // 8, 4)), 4)
        z = lax.rem(zz + far(lax.rem(t // 2, 4)), 4)
        c = lax.rem(cc + 1 + lax.rem(t, 2), 2)
        return (y * 4 + x, z * 2 + c)

    loads = [
        pltpu.make_async_copy(f_hbm, fv, hsem.at[0]),
        pltpu.make_async_copy(modes_hbm, mv, hsem.at[1]),
        pltpu.make_async_copy(coarse_hbm, crows.at[pl.ds(0, 16)], hsem.at[2]),
    ]
    big = [
        pltpu.make_async_copy(mat.at[s], stage.at[2 * n + s], hsem.at[3 + 2 * n + s])
        for n, mat in enumerate((precond_hbm, schur_hbm))
        for s in range(2)
    ]
    for copy in loads + big:
        copy.start()

    barrier = pltpu.get_barrier_semaphore()

    def greet(t, carry):
        pl.semaphore_signal(barrier, inc=1, device_id=other(t), device_id_type=MESH)
        return carry

    lax.fori_loop(0, 127, greet, 0)

    def classify(b, carry):
        s, n = nsub_ref[b // 8, lax.rem(b, 8)], nblk_ref[b // 8, lax.rem(b, 8)]
        dev = s // 2
        dsub, dblk = dev // NBLK_AX, lax.rem(dev, NBLK_AX)
        g = jnp.where(
            dsub == around[0][0], 0,
            jnp.where(dsub == around[1][0], 1, jnp.where(dblk == around[2][1], 2, 3)),
        )
        theirs = lax.rem(s, 2) * 8 + n
        g = jnp.where(s < 0, 4, g)
        group[b] = jnp.where(s < 0, 8, 2 * g + lax.rem(s, 2))
        key[b] = g * 16 + jnp.where((g == 1) | (g == 3), theirs, b)
        return carry

    lax.fori_loop(0, 16, classify, 0)

    def place(b, carry):
        mine = key[b]
        g = mine // 16

        def count(o, slot):
            k = key[o]
            return slot + jnp.where((k < mine) & (k // 16 == g), 1, 0)

        slot = lax.fori_loop(0, 16, count, jnp.int32(0), unroll=True)
        source[b] = jnp.where(g == 4, 16, g * 4 + jnp.minimum(slot, 3))
        return carry

    lax.fori_loop(0, 16, place, 0)

    def invert(t, carry):
        def match(b, found):
            return jnp.where(source[b] == t, b, found)

        pick[t] = lax.fori_loop(0, 16, match, jnp.int32(0), unroll=True)
        return carry

    lax.fori_loop(0, 16, invert, 0)

    for copy in loads:
        copy.wait()

    zero = jnp.zeros((8, 128), F32)
    pad = jnp.zeros((2, 128), F32)
    for b in range(16):
        s, cols = b // 8, slice((b % 8) * 128, (b % 8) * 128 + 128)
        wide = slice(b * 128, b * 128 + 128)
        wblk[b] = fv[s, :, cols]
        m8 = jnp.concatenate([mv[s, :, cols], pad], axis=0)
        mown[b] = m8
        rows = jnp.concatenate([m8, zero] if s == 0 else [zero, m8], axis=0)
        h, l = split(rows)
        ghi[:, wide] = h
        glo[:, wide] = l
        aghi[0:16, wide] = h
        aglo[0:16, wide] = l
    row = lax.broadcasted_iota(jnp.int32, (16, 128), 0)
    ghi[:, 2048:2176] = jnp.where(row == 6, 1.0, 0.0).astype(BF16)
    glo[:, 2048:2176] = jnp.zeros((16, 128), BF16)
    for t in range(16):
        fsend[t] = wblk[pick[t]]
        msend[t] = mown[pick[t]]
    frecv[16] = jnp.zeros((16, 128), F32)
    for buf in wrecv:
        buf[16] = jnp.zeros((16, 128), F32)

    def halve(n, s, hi_ref, lo_ref):
        def step(t, carry):
            rows = pl.ds(pl.multiple_of(t * 32, 32), 32)
            h, l = split(stage[2 * n + s, rows])
            hi_ref[s, rows] = h
            lo_ref[s, rows] = l
            return carry

        big[2 * n + s].wait()
        lax.fori_loop(0, 32, step, 0)

    halve(0, 0, khi, klo)
    halve(0, 1, khi, klo)

    pl.semaphore_wait(barrier, 127)

    first = []
    for g, where in enumerate(around):
        there = g ^ 1
        for n, (src, dst) in enumerate((
            (fsend.at[pl.ds(4 * g, 4)], frecv.at[pl.ds(4 * there, 4)]),
            (msend.at[pl.ds(4 * g, 4)], mrecv.at[pl.ds(4 * there, 4)]),
            (crows.at[pl.ds(0, 16)], crows.at[pl.ds(16 + 16 * there, 16)]),
        )):
            copy = pltpu.make_async_remote_copy(
                src, dst, ssem0.at[3 * g + n], rsem0.at[3 * there + n], where, MESH
            )
            copy.start()
            first.append((n, copy))

    halve(1, 0, shi, slo)

    for n, copy in first:
        if n < 2:
            copy.wait_recv()
    for b in range(16):
        wide = slice(b * 128, b * 128 + 128)
        res[:, wide] = wblk[b] - frecv[source[b]]
        theirs = mrecv[lax.rem(source[b], 16)]
        code = group[b]
        for pair in range(4):
            both = jnp.concatenate(
                [jnp.where(code == 2 * pair + s2, -theirs, 0.0) for s2 in range(2)], axis=0
            )
            h, l = split(both)
            rows = slice(16 + 16 * pair, 32 + 16 * pair)
            aghi[rows, wide] = h
            aglo[rows, wide] = l

    lane = lax.broadcasted_iota(jnp.int32, (16, 128), 1)
    own = (lane // 16) == lax.rem(row, 8)

    def payload(vec, scalar):
        u = jnp.concatenate([vec, scalar], axis=1)
        uh, ul = split(u)
        uh = jnp.concatenate([uh] * 8, axis=0)
        ul = jnp.concatenate([ul] * 8, axis=0)
        both = dot_t(jnp.concatenate([ghi[...], glo[...]], axis=0), uh)
        r = both[:16] + both[16:] + dot_t(ghi[...], ul)
        r = jnp.where(own, r, 0.0)
        return jnp.sum(r.reshape(2, 8, 128), axis=1)

    def spread_out(k, value):
        mine = gath.at[k, me]
        gath[k, me] = value

        def send(t, carry):
            pltpu.make_async_remote_copy(
                mine, mine, ssemg.at[k], rsemg.at[k], other(t), MESH
            ).start()
            return carry

        lax.fori_loop(0, 127, send, 0)

    def wait_all(sem, k):
        many = gath.at[k, pl.ds(0, 127)]
        pltpu.make_async_copy(many, many, sem.at[k]).wait()

    def factors(k):
        wait_all(rsemg, k)
        x = gath.at[k].reshape(256, 128)[...].T
        left = jnp.concatenate([x[16 * m : 16 * m + 16] for m in range(6)], axis=1)
        scalar = jnp.sum(x[96:112], axis=1, keepdims=True)
        return product3(left, chi[...], clo[...], dot_t), scalar

    def apply(hi_ref, lo_ref, s, vec, store):
        for q in range(4):
            cols = slice(q * 256, q * 256 + 256)
            store(
                slice(s * 1024 + q * 256, s * 1024 + q * 256 + 256),
                product3(vec, hi_ref[s, :, cols], lo_ref[s, :, cols]),
            )

    swaps = []

    def swap(k):
        for t in range(16):
            wsend[k, t] = wblk[pick[t]]
        copies = []
        for g, where in enumerate(around):
            there = g ^ 1
            copy = pltpu.make_async_remote_copy(
                wsend.at[k, pl.ds(4 * g, 4)], wrecv[k].at[pl.ds(4 * there, 4)],
                ssemx.at[k, g], rsemx.at[k, there], where, MESH,
            )
            copy.start()
            copies.append(copy)
        for copy in copies:
            copy.wait_recv()
        swaps.extend(copies)

    def assembled(k, b):
        return wblk[b] - wrecv[k][source[b]]

    def block_sum(a, b):
        total = a[:, 0:128] * b[:, 0:128]
        for n in range(1, 16):
            cols = slice(n * 128, n * 128 + 128)
            total = total + a[:, cols] * b[:, cols]
        return total

    def put_blocks(x):
        for b in range(16):
            wblk[b] = x[:, b * 128 : b * 128 + 128]

    spread_out(0, payload(res[...], jnp.zeros((16, 128), F32)))

    halve(1, 1, shi, slo)
    for n, copy in first:
        if n == 2:
            copy.wait_recv()
    h, l = split(crows[...])
    chi[...] = h
    clo[...] = l

    def apply_first(hi_ref, lo_ref, out_hi, out_lo, vec_ref, vec_out):
        for s in range(2):
            cols = slice(s * 1024, s * 1024 + 1024)
            ah, al = aghi[:, cols], aglo[:, cols]
            parts_hi, parts_lo = [ah], [al]
            if vec_ref is not None:
                vh, vl = split(vec_ref[:, cols])
                parts_hi, parts_lo = [vh, ah], [vl, al]
            lh = jnp.concatenate(parts_hi, axis=0)
            ll = jnp.concatenate(parts_lo, axis=0)
            n = lh.shape[0]
            lhl = jnp.concatenate([lh, ll], axis=0)
            for q in range(4):
                c = slice(q * 256, q * 256 + 256)
                o = slice(s * 1024 + q * 256, s * 1024 + q * 256 + 256)
                both = dot(lhl, hi_ref[s, :, c])
                total = both[:n] + both[n:] + dot(lh, lo_ref[s, :, c])
                if vec_ref is not None:
                    vec_out[:, o] = total[:16]
                    total = total[16:]
                oh, ol = split(total)
                out_hi[:, o] = oh
                out_lo[:, o] = ol

    apply_first(khi, klo, kaghi, kaglo, res, kres)
    apply_first(shi, slo, saghi, saglo, None, None)

    fr, _ = factors(0)
    fres[...] = fr
    rho_before = None
    for it in range(ITERS):
        fr = fres[...]
        p = res[...] - product3(fr, aghi[...], aglo[...])
        w = kres[...] - product3(fr, kaghi[...], kaglo[...])
        put_blocks(w)
        part = block_sum(w, p)
        swap(2 * it)
        for b in range(16):
            zvec[:, b * 128 : b * 128 + 128] = assembled(2 * it, b)
        spread_out(1 + 2 * it, payload(zvec[...], part))
        for s in range(2):
            def store(cols, value):
                szvec[:, cols] = value

            apply(shi, slo, s, zvec[:, s * 1024 : s * 1024 + 1024], store)
        fz, rho = factors(1 + 2 * it)
        y = zvec[...] - product3(fz, aghi[...], aglo[...])
        q = szvec[...] - product3(fz, saghi[...], saglo[...])
        if it > 0:
            beta = rho / rho_before
            y = y + beta * dirv[...]
            q = q + beta * qvec[...]
        dirv[...] = y
        qvec[...] = q
        put_blocks(q)
        part = block_sum(q, y)
        swap(2 * it + 1)
        for b in range(16):
            zvec[:, b * 128 : b * 128 + 128] = assembled(2 * it + 1, b)
        spread_out(2 + 2 * it, payload(zvec[...], part))
        if it + 1 < ITERS:
            for s in range(2):
                def store(cols, value):
                    szvec[:, cols] = value

                apply(khi, klo, s, zvec[:, s * 1024 : s * 1024 + 1024], store)
        fi, sigma = factors(2 + 2 * it)
        step = rho / sigma
        for s in range(2):
            cols = slice(s * 1024, s * 1024 + 1024)
            add = step * dirv[:, cols]
            if it == 0:
                lam_ref[s] = add
            else:
                lam_ref[s] += add
        res[...] = res[...] - step * zvec[...]
        if it + 1 < ITERS:
            kres[...] = kres[...] - step * szvec[...]
        fres[...] = fres[...] - step * fi
        rho_before = rho

    p = res[...] - product3(fres[...], aghi[...], aglo[...])
    for s in range(2):
        out_ref[s] = p[:, s * 1024 : s * 1024 + 1024]

    for _, copy in first:
        copy.wait_send()
    for copy in swaps:
        copy.wait_send()
    for k in range(GATHERS):
        wait_all(ssemg, k)


def per_device(f_local, schur, precond, modes, coarse_inv, nbr_sub, nbr_blk):
    rows = coarse_inv.reshape(2, 6, 256, 6).transpose(0, 1, 3, 2).reshape(2, 6, 1536)
    rows = jnp.pad(rows, ((0, 0), (0, 2), (0, 0))).reshape(16, 1536)
    dma = pltpu.SemaphoreType.DMA
    vec = pltpu.VMEM((16, 2048), F32)
    out = jax.ShapeDtypeStruct((2, 16, 1024), F32)
    anywhere = pl.BlockSpec(memory_space=pl.ANY)
    smem = pl.BlockSpec(memory_space=pltpu.SMEM)
    half = pltpu.VMEM((2, 1024, 1024), BF16)
    tall = pltpu.VMEM((ROWS, 2048), BF16)
    blocks = pltpu.VMEM((17, 16, 128), F32)
    table = pltpu.SMEM((16,), jnp.int32)
    return pl.pallas_call(
        kernel,
        out_shape=(out, out),
        in_specs=[smem, smem] + [anywhere] * 5,
        out_specs=(pl.BlockSpec(memory_space=pltpu.VMEM),) * 2,
        scratch_shapes=[
            pltpu.VMEM((2, 16, 1024), F32), pltpu.VMEM((2, 6, 1024), F32),
            pltpu.VMEM((4, 1024, 1024), F32), half, half, half, half,
            table, table, table, table,
            pltpu.VMEM((16, 16, 128), F32), pltpu.VMEM((17, 16, 128), F32),
            pltpu.VMEM((16, 8, 128), F32), pltpu.VMEM((16, 8, 128), F32), pltpu.VMEM((16, 8, 128), F32),
            pltpu.VMEM((ROWS, 1536), F32),
            pltpu.VMEM((ROWS, 1536), BF16), pltpu.VMEM((ROWS, 1536), BF16),
            tall, tall, tall, tall, tall, tall,
            pltpu.VMEM((16, 2176), BF16), pltpu.VMEM((16, 2176), BF16),
            pltpu.VMEM((SWAPS, 16, 16, 128), F32), blocks, blocks, blocks, blocks,
            pltpu.VMEM((16, 16, 128), F32),
            pltpu.VMEM((GATHERS, 128, 2, 128), F32),
            vec, vec, vec, vec, vec, vec,
            pltpu.VMEM((16, ROWS), F32),
            dma((7,)), dma((12,)), dma((12,)), dma((SWAPS, 4)), dma((SWAPS, 4)),
            dma((GATHERS,)), dma((GATHERS,)),
        ],
        compiler_params=pltpu.CompilerParams(
            collective_id=0, has_side_effects=True, vmem_limit_bytes=56 * 2**20
        ),
        cost_estimate=pl.CostEstimate(flops=10**9, bytes_accessed=2 * 10**7, transcendentals=0),
    )(nbr_sub, nbr_blk, f_local, schur, precond, modes, rows)


def solution(mesh):
    flat = P(("sub", "blk"), None)
    tall = P(("sub", "blk"), None, None)
    return jax.shard_map(
        per_device,
        mesh=mesh,
        in_specs=(tall, tall, tall, tall, flat, flat, flat),
        out_specs=(tall, tall),
        check_vma=False,
    )
```

time: 623 us -> 105 us (0.17); the launches traced: 614 us -> 105 us
  blocking collectives: 375 us -> 0 us
  waiting for transfers between devices: 126 us -> 0 us
  Pallas kernels: 0 us -> 95.7 us
  starting transfers between devices: 49.6 us -> 0 us
  matrix products: 43 us -> 0 us
  other arithmetic: 7.4 us -> 0 us
    psum x3 -> x0, blocking collectives: 193 us -> none  [the longest x2 128 us: per_device(): rho_now = lax.psum(weighted_dot(search, residual, weights), ('sub', 'blk'))]
    all_gather x5 -> x0, blocking collectives: 182 us -> none  [coarse_factors(): every_moment = lax.all_gather(moments, ('sub', 'blk'), axis=1, tiled=True)]
    ppermute x40 -> x0, waiting for transfers between devices: 126 us -> none  [the longest x20 79.6 us: with_halo(): lax.ppermute(head, axis, [((i + 1) % count, i) for i in range(count)])]
    pallas_call x0 -> x1, Pallas kernels: none -> 95.7 us  [per_device(): pl.pallas_call(kernel, out_shape=(out, out), in_specs=[smem, smem] + [any...]
    ppermute x40 -> x0, starting transfers between devices: 49.6 us -> none  [the longest x20 42.3 us: with_halo(): lax.ppermute(head, axis, [((i + 1) % count, i) for i in range(count)])]
    dot_general x19 -> x0, matrix products: 43 us -> none  [the longest x4 37.1 us: apply_local(): jnp.einsum('sij,scj->sci', matrices, values, precision=lax.Precision.HIGH...]
  transfers between devices with their start and end apart: 40 -> 0, of which waited for: 30 -> 0; matrix products, arithmetic and copies ran while one was open for 0% -> 0% of each run, Pallas kernels for 0% -> 0%
where the time goes in v1:
time: 105 us
  Pallas kernels  95.7 us (91%)
  local copies, waits for them, and re-layouts  8.21 us (8%)
    pallas_call x1, Pallas kernels, per_device(): pl.pallas_call(kernel, out_shape=(out, out), in_specs=[smem, smem] + [any...  95.7 us
    unnamed x5, local copies, waits for them, and re-layouts  5.09 us
    reshape x1, local copies, waits for them, and re-layouts, per_device(): coarse_inv.reshape(2, 6, 256, 6).transpose(0, 1, 3, 2).reshape(2, 6, 1536)  2.47 us

profile of v1, /device:TPU:1, one launch (start us, length us, event | category | flops | bytes accessed | tf_op | source)
XLA Modules:
  0.0 104.5 jit_solution(10373035299908259035)
XLA Ops:
  0.6 2.5 %reshape.13 = f32[2,6,256,6]{3,2,1,0:T(8,128)S(1)} reshape(f32[12,1536]{1,0:T(8,128)} %param.11) | data formatting | bytes 147456 | tf_op jit(solution)/shard_map/reshape | solution.py:385
  3.1 0.5 copy.15
  3.6 0.6 pad_bitcast_fusion.coarse_hbm
  4.3 1.4 %copy.13.modes_hbm = f32[2,6,1024]{2,1,0:T(8,128)} copy(f32[2,6,1024]{2,0,1:T(2,128)} %param.10) | data formatting | bytes 98304 | tf_op args[3]
  5.7 95.7 %shard_map.86 = (f32[2,16,1024]{2,1,0:T(8,128)}, f32[2,16,1024]{2,1,0:T(8,128)}) custom-call(s32[2,8]{1,0:T(2,128)} %nsub_ref.1, s32[2,8]{1,0:T(2,128)} %nblk_ref.1, f32[2,16,1024]{2,1,0:T(8,128)} %f_hbm.1, f32[2,1024,1024]{2,1,0:T(8,128)} %schur_hbm.1, f32[2,1024,1024]{2,1,0:T(8,128)} %precond_hbm.1, f32[2,6,1024]{2,1,0:T(8,128)} %copy.13.modes_hbm, ...), custom_call_target="tpu_custom_call" | custom-call | flops 1000000000 | bytes 20000000 | tf_op jit(solution)/shard_map/pallas_call | solution.py:396
  101.4 1.6 %copy.19 = f32[2,16,1024]{2,1,0:T(8,128)} copy(f32[2,16,1024]{2,1,0:T(8,128)} %get-tuple-element.4) | data formatting | bytes 262144
  103.0 1.6 %copy.20 = f32[2,16,1024]{2,1,0:T(8,128)} copy(f32[2,16,1024]{2,1,0:T(8,128)} %get-tuple-element.5) | data formatting | bytes 262144
  (1 shorter events, 0.0 us)

commit v2 on v1

--- a/solution.py
+++ b/solution.py
@@ -37,9 +37,9 @@
 def kernel(
     nsub_ref, nblk_ref, f_hbm, schur_hbm, precond_hbm, modes_hbm, coarse_hbm,
     lam_ref, out_ref,
-    fv, mv, stage, khi, klo, shi, slo,
+    fv, mv, craw, cpad, order, stage, khi, klo, shi, slo,
     group, key, source, pick,
-    fsend, frecv, mown, msend, mrecv, crows, chi, clo,
+    fsend, frecv, mown, msend, mrecv, crows, cboth,
     aghi, aglo, kaghi, kaglo, saghi, saglo, ghi, glo,
     wsend, wrecv0, wrecv1, wrecv2, wrecv3, wblk, gath,
     res, kres, zvec, szvec, dirv, qvec, fres,
@@ -59,17 +59,26 @@
     def far(q):
         return 2 + (q * (q + 1)) // 2
 
-    def other(t):
-        y = lax.rem(yy + far(t // 32), 4)
-        x = lax.rem(xx + far(lax.rem(t // 8, 4)), 4)
-        z = lax.rem(zz + far(lax.rem(t // 2, 4)), 4)
-        c = lax.rem(cc + 1 + lax.rem(t, 2), 2)
-        return (y * 4 + x, z * 2 + c)
+    columns = [
+        lax.rem(zz + dz, 4) * 2 + lax.rem(cc + dc, 2) for dz in (2, 1, 3, 0) for dc in (1, 0)
+    ]
+
+    def each_other(act):
+        def row(t, carry):
+            y = lax.rem(yy + far(t // 4), 4)
+            x = lax.rem(xx + far(lax.rem(t, 4)), 4)
+            for column in columns:
+                act((y * 4 + x, column))
+            return carry
+
+        lax.fori_loop(0, 15, row, 0)
+        for column in columns[:-1]:
+            act((i, column))
 
     loads = [
         pltpu.make_async_copy(f_hbm, fv, hsem.at[0]),
         pltpu.make_async_copy(modes_hbm, mv, hsem.at[1]),
-        pltpu.make_async_copy(coarse_hbm, crows.at[pl.ds(0, 16)], hsem.at[2]),
+        pltpu.make_async_copy(coarse_hbm, craw, hsem.at[2]),
     ]
     big = [
         pltpu.make_async_copy(mat.at[s], stage.at[2 * n + s], hsem.at[3 + 2 * n + s])
@@ -81,11 +90,9 @@
 
     barrier = pltpu.get_barrier_semaphore()
 
-    def greet(t, carry):
-        pl.semaphore_signal(barrier, inc=1, device_id=other(t), device_id_type=MESH)
-        return carry
-
-    lax.fori_loop(0, 127, greet, 0)
+    each_other(
+        lambda where: pl.semaphore_signal(barrier, inc=1, device_id=where, device_id_type=MESH)
+    )
 
     def classify(b, carry):
         s, n = nsub_ref[b // 8, lax.rem(b, 8)], nblk_ref[b // 8, lax.rem(b, 8)]
@@ -135,7 +142,7 @@
         s, cols = b // 8, slice((b % 8) * 128, (b % 8) * 128 + 128)
         wide = slice(b * 128, b * 128 + 128)
         wblk[b] = fv[s, :, cols]
-        m8 = jnp.concatenate([mv[s, :, cols], pad], axis=0)
+        m8 = jnp.concatenate([mv[:, s, cols], pad], axis=0)
         mown[b] = m8
         rows = jnp.concatenate([m8, zero] if s == 0 else [zero, m8], axis=0)
         h, l = split(rows)
@@ -143,26 +150,41 @@
         glo[:, wide] = l
         aghi[0:16, wide] = h
         aglo[0:16, wide] = l
+    col = lax.broadcasted_iota(jnp.int32, (1, 768), 1)
+    wanted = 6 * lax.rem(col, 128) + col // 128
+    for n in range(6):
+        rows = slice(n * 128, n * 128 + 128)
+        here = lax.broadcasted_iota(jnp.int32, (128, 768), 0) + n * 128
+        order[rows] = jnp.where(here == wanted, 1.0, 0.0).astype(BF16)
+    cpad[...] = jnp.zeros((16, 1536), F32)
+    cpad[0:6] = craw[0:6]
+    cpad[8:14] = craw[6:12]
+    for h in range(2):
+        cols = slice(768 * h, 768 * h + 768)
+        ch, cl = split(cpad[:, cols])
+        both = dot(jnp.concatenate([ch, cl], axis=0), order[...])
+        crows[0:16, cols] = both[:16] + both[16:]
     row = lax.broadcasted_iota(jnp.int32, (16, 128), 0)
     ghi[:, 2048:2176] = jnp.where(row == 6, 1.0, 0.0).astype(BF16)
     glo[:, 2048:2176] = jnp.zeros((16, 128), BF16)
     for t in range(16):
         fsend[t] = wblk[pick[t]]
         msend[t] = mown[pick[t]]
+    crows[ROWS:128] = jnp.zeros((128 - ROWS, 1536), F32)
     frecv[16] = jnp.zeros((16, 128), F32)
     for buf in wrecv:
         buf[16] = jnp.zeros((16, 128), F32)
 
     def halve(n, s, hi_ref, lo_ref):
         def step(t, carry):
-            rows = pl.ds(pl.multiple_of(t * 32, 32), 32)
+            rows = pl.ds(pl.multiple_of(t * 64, 64), 64)
             h, l = split(stage[2 * n + s, rows])
             hi_ref[s, rows] = h
             lo_ref[s, rows] = l
             return carry
 
         big[2 * n + s].wait()
-        lax.fori_loop(0, 32, step, 0)
+        lax.fori_loop(0, 16, step, 0, unroll=2)
 
     halve(0, 0, khi, klo)
     halve(0, 1, khi, klo)
@@ -219,13 +241,11 @@
         mine = gath.at[k, me]
         gath[k, me] = value
 
-        def send(t, carry):
-            pltpu.make_async_remote_copy(
-                mine, mine, ssemg.at[k], rsemg.at[k], other(t), MESH
+        each_other(
+            lambda where: pltpu.make_async_remote_copy(
+                mine, mine, ssemg.at[k], rsemg.at[k], where, MESH
             ).start()
-            return carry
-
-        lax.fori_loop(0, 127, send, 0)
+        )
 
     def wait_all(sem, k):
         many = gath.at[k, pl.ds(0, 127)]
@@ -234,9 +254,19 @@
     def factors(k):
         wait_all(rsemg, k)
         x = gath.at[k].reshape(256, 128)[...].T
-        left = jnp.concatenate([x[16 * m : 16 * m + 16] for m in range(6)], axis=1)
         scalar = jnp.sum(x[96:112], axis=1, keepdims=True)
-        return product3(left, chi[...], clo[...], dot_t), scalar
+        left = jnp.concatenate(
+            [
+                jnp.concatenate(
+                    [part[16 * m : 16 * m + 16, 128 * h : 128 * h + 128] for h in range(2) for m in range(6)],
+                    axis=1,
+                )
+                for part in split(x)
+            ],
+            axis=0,
+        )
+        both = dot(left, cboth[...])
+        return (both[:16, :128] + both[16:, :128] + both[:16, 128:])[:, :ROWS], scalar
 
     def apply(hi_ref, lo_ref, s, vec, store):
         for q in range(4):
@@ -284,9 +314,9 @@
     for n, copy in first:
         if n == 2:
             copy.wait_recv()
-    h, l = split(crows[...])
-    chi[...] = h
-    clo[...] = l
+    h, l = split(crows[...].T)
+    cboth[:, 0:128] = h
+    cboth[:, 128:256] = l
 
     def apply_first(hi_ref, lo_ref, out_hi, out_lo, vec_ref, vec_out):
         for s in range(2):
@@ -382,8 +412,6 @@
 
 
 def per_device(f_local, schur, precond, modes, coarse_inv, nbr_sub, nbr_blk):
-    rows = coarse_inv.reshape(2, 6, 256, 6).transpose(0, 1, 3, 2).reshape(2, 6, 1536)
-    rows = jnp.pad(rows, ((0, 0), (0, 2), (0, 0))).reshape(16, 1536)
     dma = pltpu.SemaphoreType.DMA
     vec = pltpu.VMEM((16, 2048), F32)
     out = jax.ShapeDtypeStruct((2, 16, 1024), F32)
@@ -399,13 +427,13 @@
         in_specs=[smem, smem] + [anywhere] * 5,
         out_specs=(pl.BlockSpec(memory_space=pltpu.VMEM),) * 2,
         scratch_shapes=[
-            pltpu.VMEM((2, 16, 1024), F32), pltpu.VMEM((2, 6, 1024), F32),
+            pltpu.VMEM((2, 16, 1024), F32), pltpu.VMEM((6, 2, 1024), F32),
+            pltpu.VMEM((12, 1536), F32), pltpu.VMEM((16, 1536), F32), pltpu.VMEM((768, 768), BF16),
             pltpu.VMEM((4, 1024, 1024), F32), half, half, half, half,
             table, table, table, table,
             pltpu.VMEM((16, 16, 128), F32), pltpu.VMEM((17, 16, 128), F32),
             pltpu.VMEM((16, 8, 128), F32), pltpu.VMEM((16, 8, 128), F32), pltpu.VMEM((16, 8, 128), F32),
-            pltpu.VMEM((ROWS, 1536), F32),
-            pltpu.VMEM((ROWS, 1536), BF16), pltpu.VMEM((ROWS, 1536), BF16),
+            pltpu.VMEM((128, 1536), F32), pltpu.VMEM((1536, 256), BF16),
             tall, tall, tall, tall, tall, tall,
             pltpu.VMEM((16, 2176), BF16), pltpu.VMEM((16, 2176), BF16),
             pltpu.VMEM((SWAPS, 16, 16, 128), F32), blocks, blocks, blocks, blocks,
@@ -420,7 +448,7 @@
             collective_id=0, has_side_effects=True, vmem_limit_bytes=56 * 2**20
         ),
         cost_estimate=pl.CostEstimate(flops=10**9, bytes_accessed=2 * 10**7, transcendentals=0),
-    )(nbr_sub, nbr_blk, f_local, schur, precond, modes, rows)
+    )(nbr_sub, nbr_blk, f_local, schur, precond, modes.transpose(1, 0, 2), coarse_inv)
 
 
 def solution(mesh):

time: 105 us -> 77.1 us (0.73)
  Pallas kernels: 95.7 us -> 73.2 us
  local copies, waits for them, and re-layouts: 8.21 us -> 3.14 us
    pallas_call x1, Pallas kernels: 95.7 us -> 73.2 us  [per_device(): pl.pallas_call(kernel, out_shape=(out, out), in_specs=[smem, smem] + [any...]
    reshape x2 -> x0, local copies, waits for them, and re-layouts: 3.12 us -> none  [the longest x1 2.47 us: per_device(): coarse_inv.reshape(2, 6, 256, 6).transpose(0, 1, 3, 2).reshape(2, 6, 1536)]
    unnamed x5 -> x2, local copies, waits for them, and re-layouts: 5.09 us -> 3.14 us
where the time goes in v2:
time: 77.1 us; the launch traced here: 77 us
  Pallas kernels  73.2 us (95%)
  local copies, waits for them, and re-layouts  3.14 us (4%)
    pallas_call x1, Pallas kernels, per_device(): pl.pallas_call(kernel, out_shape=(out, out), in_specs=[smem, smem] + [any...  73.2 us
    unnamed x2, local copies, waits for them, and re-layouts  3.14 us

profile of v2, /device:TPU:1, one launch (start us, length us, event | category | flops | bytes accessed | tf_op | source)
XLA Modules:
  0.0 77.0 jit_solution(16950296035808713702)
XLA Ops:
  0.6 73.2 %shard_map.86 = (f32[2,16,1024]{2,1,0:T(8,128)}, f32[2,16,1024]{2,1,0:T(8,128)}) custom-call(s32[2,8]{1,0:T(2,128)} %nsub_ref.1, s32[2,8]{1,0:T(2,128)} %nblk_ref.1, f32[2,16,1024]{2,1,0:T(8,128)} %f_hbm.1, f32[2,1024,1024]{2,1,0:T(8,128)} %schur_hbm.1, f32[2,1024,1024]{2,1,0:T(8,128)} %precond_hbm.1, f32[6,2,1024]{2,1,0:T(2,128)} %bitcast.1, ...), custom_call_target="tpu_custom_call" | custom-call | flops 1000000000 | bytes 20000000 | tf_op jit(solution)/shard_map/pallas_call | solution.py:424
  73.8 1.6 %copy.11 = f32[2,16,1024]{2,1,0:T(8,128)} copy(f32[2,16,1024]{2,1,0:T(8,128)} %get-tuple-element.4) | data formatting | bytes 262144
  75.4 1.6 %copy.12 = f32[2,16,1024]{2,1,0:T(8,128)} copy(f32[2,16,1024]{2,1,0:T(8,128)} %get-tuple-element.5) | data formatting | bytes 262144

commit v3 on v2

--- a/solution.py
+++ b/solution.py
@@ -10,6 +10,7 @@
 SWAPS = 2 * ITERS
 NSUB_AX, NBLK_AX = 16, 8
 ROWS = 80
+BACK = (1, 0, 2, 3)
 MESH = pl.DeviceIdType.MESH
 F32, BF16 = jnp.float32, jnp.bfloat16
 
@@ -40,30 +41,28 @@
     fv, mv, craw, cpad, order, stage, khi, klo, shi, slo,
     group, key, source, pick,
     fsend, frecv, mown, msend, mrecv, crows, cboth,
-    aghi, aglo, kaghi, kaglo, saghi, saglo, ghi, glo,
-    wsend, wrecv0, wrecv1, wrecv2, wrecv3, wblk, gath,
+    aghi, aglo, kaghi, kaglo, saghi, saglo,
+    wsend, wrecv0, wrecv1, wrecv2, wrecv3, wblk, gath, fpart, fmate,
     res, kres, zvec, szvec, dirv, qvec, fres,
-    hsem, ssem0, rsem0, ssemx, rsemx, ssemg, rsemg,
+    hsem, ssem0, rsem0, ssemx, rsemx, ssemg, rsemg, ssemf, rsemf,
 ):
     i, j = lax.axis_index("sub"), lax.axis_index("blk")
-    me = i * NBLK_AX + j
     wrecv = (wrecv0, wrecv1, wrecv2, wrecv3)
     yy, xx, zz, cc = i // 4, lax.rem(i, 4), j // 2, lax.rem(j, 2)
     around = [
         (lax.rem(i + 1, NSUB_AX), j),
         (lax.rem(i + NSUB_AX - 1, NSUB_AX), j),
-        (i, lax.rem(j + 1, NBLK_AX)),
-        (i, lax.rem(j + NBLK_AX - 1, NBLK_AX)),
+        (i, lax.rem(j + NBLK_AX - 1 + 2 * cc, NBLK_AX)),
+        (i, j + 1 - 2 * cc),
     ]
+    slot = i * 4 + zz
 
     def far(q):
         return 2 + (q * (q + 1)) // 2
 
-    columns = [
-        lax.rem(zz + dz, 4) * 2 + lax.rem(cc + dc, 2) for dz in (2, 1, 3, 0) for dc in (1, 0)
-    ]
-
-    def each_other(act):
+    columns = [lax.rem(zz + dz, 4) * 2 + cc for dz in (2, 1, 3, 0)]
+
+    def each_chip(act):
         def row(t, carry):
             y = lax.rem(yy + far(t // 4), 4)
             x = lax.rem(xx + far(lax.rem(t, 4)), 4)
@@ -90,9 +89,12 @@
 
     barrier = pltpu.get_barrier_semaphore()
 
-    each_other(
-        lambda where: pl.semaphore_signal(barrier, inc=1, device_id=where, device_id_type=MESH)
-    )
+    def greet(where):
+        pl.semaphore_signal(barrier, inc=1, device_id=where, device_id_type=MESH)
+
+    each_chip(greet)
+    greet(around[2])
+    greet(around[3])
 
     def classify(b, carry):
         s, n = nsub_ref[b // 8, lax.rem(b, 8)], nblk_ref[b // 8, lax.rem(b, 8)]
@@ -105,12 +107,13 @@
         theirs = lax.rem(s, 2) * 8 + n
         g = jnp.where(s < 0, 4, g)
         group[b] = jnp.where(s < 0, 8, 2 * g + lax.rem(s, 2))
-        key[b] = g * 16 + jnp.where((g == 1) | (g == 3), theirs, b)
+        mine = (g == 0) | (g == 4) | ((g >= 2) & (cc == 0))
+        key[b] = g * 16 + jnp.where(mine, b, theirs)
         return carry
 
     lax.fori_loop(0, 16, classify, 0)
 
-    def place(b, carry):
+    def rank(b, carry):
         mine = key[b]
         g = mine // 16
 
@@ -122,7 +125,7 @@
         source[b] = jnp.where(g == 4, 16, g * 4 + jnp.minimum(slot, 3))
         return carry
 
-    lax.fori_loop(0, 16, place, 0)
+    lax.fori_loop(0, 16, rank, 0)
 
     def invert(t, carry):
         def match(b, found):
@@ -146,12 +149,12 @@
         mown[b] = m8
         rows = jnp.concatenate([m8, zero] if s == 0 else [zero, m8], axis=0)
         h, l = split(rows)
-        ghi[:, wide] = h
-        glo[:, wide] = l
         aghi[0:16, wide] = h
         aglo[0:16, wide] = l
     col = lax.broadcasted_iota(jnp.int32, (1, 768), 1)
-    wanted = 6 * lax.rem(col, 128) + col // 128
+    spot = lax.rem(col, 128)
+    wanted = 16 * lax.rem(spot // 8, 8) + 4 * lax.rem(spot // 2, 4) + 2 * (spot // 64)
+    wanted = 6 * (wanted + lax.rem(spot, 2)) + col // 128
     for n in range(6):
         rows = slice(n * 128, n * 128 + 128)
         here = lax.broadcasted_iota(jnp.int32, (128, 768), 0) + n * 128
@@ -164,13 +167,12 @@
         ch, cl = split(cpad[:, cols])
         both = dot(jnp.concatenate([ch, cl], axis=0), order[...])
         crows[0:16, cols] = both[:16] + both[16:]
-    row = lax.broadcasted_iota(jnp.int32, (16, 128), 0)
-    ghi[:, 2048:2176] = jnp.where(row == 6, 1.0, 0.0).astype(BF16)
-    glo[:, 2048:2176] = jnp.zeros((16, 128), BF16)
+    row = lax.broadcasted_iota(jnp.int32, (ROWS, 128), 0)
+    aghi[:, 2048:2176] = jnp.where(row == 6, 1.0, 0.0).astype(BF16)
+    aglo[:, 2048:2176] = jnp.zeros((ROWS, 128), BF16)
     for t in range(16):
         fsend[t] = wblk[pick[t]]
         msend[t] = mown[pick[t]]
-    crows[ROWS:128] = jnp.zeros((128 - ROWS, 1536), F32)
     frecv[16] = jnp.zeros((16, 128), F32)
     for buf in wrecv:
         buf[16] = jnp.zeros((16, 128), F32)
@@ -186,33 +188,34 @@
         big[2 * n + s].wait()
         lax.fori_loop(0, 16, step, 0, unroll=2)
 
-    halve(0, 0, khi, klo)
-    halve(0, 1, khi, klo)
-
-    pl.semaphore_wait(barrier, 127)
-
-    first = []
-    for g, where in enumerate(around):
-        there = g ^ 1
-        for n, (src, dst) in enumerate((
-            (fsend.at[pl.ds(4 * g, 4)], frecv.at[pl.ds(4 * there, 4)]),
-            (msend.at[pl.ds(4 * g, 4)], mrecv.at[pl.ds(4 * there, 4)]),
-            (crows.at[pl.ds(0, 16)], crows.at[pl.ds(16 + 16 * there, 16)]),
-        )):
+    pl.semaphore_wait(barrier, 65)
+
+    first = [[], [], []]
+    sources = ((msend, mrecv, 4), (fsend, frecv, 4), (crows, crows, 16))
+
+    def start_first(n):
+        src, dst, size = sources[n]
+        for g, where in enumerate(around):
+            there = BACK[g]
+            if n < 2:
+                a, b = src.at[pl.ds(size * g, size)], dst.at[pl.ds(size * there, size)]
+            else:
+                a, b = src.at[pl.ds(0, 16)], dst.at[pl.ds(16 + 16 * there, 16)]
             copy = pltpu.make_async_remote_copy(
-                src, dst, ssem0.at[3 * g + n], rsem0.at[3 * there + n], where, MESH
+                a, b, ssem0.at[4 * n + g], rsem0.at[4 * n + there], where, MESH
             )
             copy.start()
-            first.append((n, copy))
-
-    halve(1, 0, shi, slo)
-
-    for n, copy in first:
-        if n < 2:
-            copy.wait_recv()
+            first[n].append(copy)
+
+    start_first(0)
+    halve(0, 0, khi, klo)
+    start_first(1)
+    start_first(2)
+    halve(0, 1, khi, klo)
+    for copy in first[0]:
+        copy.wait_recv()
     for b in range(16):
         wide = slice(b * 128, b * 128 + 128)
-        res[:, wide] = wblk[b] - frecv[source[b]]
         theirs = mrecv[lax.rem(source[b], 16)]
         code = group[b]
         for pair in range(4):
@@ -224,7 +227,7 @@
             aghi[rows, wide] = h
             aglo[rows, wide] = l
 
-    lane = lax.broadcasted_iota(jnp.int32, (16, 128), 1)
+    lane = lax.broadcasted_iota(jnp.int32, (ROWS, 128), 1)
     own = (lane // 16) == lax.rem(row, 8)
 
     def payload(vec, scalar):
@@ -232,28 +235,40 @@
         uh, ul = split(u)
         uh = jnp.concatenate([uh] * 8, axis=0)
         ul = jnp.concatenate([ul] * 8, axis=0)
-        both = dot_t(jnp.concatenate([ghi[...], glo[...]], axis=0), uh)
-        r = both[:16] + both[16:] + dot_t(ghi[...], ul)
+        both = dot_t(jnp.concatenate([aghi[...], aglo[...]], axis=0), uh)
+        r = both[:ROWS] + both[ROWS:] + dot_t(aghi[...], ul)
         r = jnp.where(own, r, 0.0)
-        return jnp.sum(r.reshape(2, 8, 128), axis=1)
+        return jnp.sum(r.reshape(5, 2, 8, 128), axis=2)
 
     def spread_out(k, value):
-        mine = gath.at[k, me]
-        gath[k, me] = value
-
-        each_other(
+        mine = gath.at[k, :, slot]
+        gath[k, :, slot] = value
+        each_chip(
             lambda where: pltpu.make_async_remote_copy(
                 mine, mine, ssemg.at[k], rsemg.at[k], where, MESH
             ).start()
         )
 
     def wait_all(sem, k):
-        many = gath.at[k, pl.ds(0, 127)]
+        many = gath.at[k, :, pl.ds(0, 63)]
         pltpu.make_async_copy(many, many, sem.at[k]).wait()
+
+    mates = []
 
     def factors(k):
         wait_all(rsemg, k)
-        x = gath.at[k].reshape(256, 128)[...].T
+        mine, plus, minus, along, mate = [gath.at[k, n].reshape(128, 128)[...] for n in range(5)]
+        same = mine + jnp.concatenate([plus[120:], plus[:120]], axis=0)
+        same = same + jnp.concatenate([minus[8:], minus[:8]], axis=0)
+        place = lax.rem(lax.broadcasted_iota(jnp.int32, (128, 128), 0), 8)
+        up = jnp.where(place < 6, pltpu.roll(along, 126, 0), pltpu.roll(along, 6, 0))
+        down = jnp.where(place >= 2, pltpu.roll(along, 2, 0), pltpu.roll(along, 122, 0))
+        other = mate + jnp.where(cc == 0, up, down)
+        first_core = jnp.where(cc == 0, same, other)
+        last_core = jnp.where(cc == 0, other, same)
+        x = jnp.concatenate(
+            [first_core[:64], last_core[:64], first_core[64:], last_core[64:]], axis=0
+        ).T
         scalar = jnp.sum(x[96:112], axis=1, keepdims=True)
         left = jnp.concatenate(
             [
@@ -266,7 +281,18 @@
             axis=0,
         )
         both = dot(left, cboth[...])
-        return (both[:16, :128] + both[16:, :128] + both[:16, 128:])[:, :ROWS], scalar
+        part = both[:16, :128] + both[16:, :128] + both[:16, 128:]
+        part = jnp.where(lane[:16] == 6, scalar, part)
+        fpart[k] = part
+        copy = pltpu.make_async_remote_copy(
+            fpart.at[k], fmate.at[k], ssemf.at[k], rsemf.at[k], around[3], MESH
+        )
+        copy.start()
+        mates.append(copy)
+        copy.wait_recv()
+        mates_part = fmate[k]
+        total = part + pltpu.roll(mates_part, 64, 1)
+        return total[:, :ROWS], part[:, 6:7] + mates_part[:, 6:7]
 
     def apply(hi_ref, lo_ref, s, vec, store):
         for q in range(4):
@@ -283,16 +309,15 @@
             wsend[k, t] = wblk[pick[t]]
         copies = []
         for g, where in enumerate(around):
-            there = g ^ 1
+            there = BACK[g]
             copy = pltpu.make_async_remote_copy(
                 wsend.at[k, pl.ds(4 * g, 4)], wrecv[k].at[pl.ds(4 * there, 4)],
                 ssemx.at[k, g], rsemx.at[k, there], where, MESH,
             )
             copy.start()
             copies.append(copy)
-        for copy in copies:
-            copy.wait_recv()
         swaps.extend(copies)
+        return copies
 
     def assembled(k, b):
         return wblk[b] - wrecv[k][source[b]]
@@ -308,15 +333,11 @@
         for b in range(16):
             wblk[b] = x[:, b * 128 : b * 128 + 128]
 
-    spread_out(0, payload(res[...], jnp.zeros((16, 128), F32)))
-
-    halve(1, 1, shi, slo)
-    for n, copy in first:
-        if n == 2:
-            copy.wait_recv()
-    h, l = split(crows[...].T)
-    cboth[:, 0:128] = h
-    cboth[:, 128:256] = l
+    spread_out(0, payload(jnp.concatenate([wblk[b] for b in range(16)], axis=1), jnp.zeros((16, 128), F32)))
+    for copy in first[1]:
+        copy.wait_recv()
+    for b in range(16):
+        res[:, b * 128 : b * 128 + 128] = wblk[b] - frecv[source[b]]
 
     def apply_first(hi_ref, lo_ref, out_hi, out_lo, vec_ref, vec_out):
         for s in range(2):
@@ -343,28 +364,43 @@
                 out_lo[:, o] = ol
 
     apply_first(khi, klo, kaghi, kaglo, res, kres)
+    for copy in first[2]:
+        copy.wait_recv()
+    hand = pltpu.make_async_remote_copy(
+        crows.at[pl.ds(16, 48)], crows.at[pl.ds(80, 48)], ssem0.at[12], rsem0.at[12], around[3], MESH
+    )
+    hand.start()
+    halve(1, 0, shi, slo)
+    halve(1, 1, shi, slo)
+
     apply_first(shi, slo, saghi, saglo, None, None)
+    hand.wait_recv()
+    h, l = split(crows[...].T)
+    cboth[:, 0:128] = h
+    cboth[:, 128:256] = l
 
     fr, _ = factors(0)
     fres[...] = fr
     rho_before = None
     for it in range(ITERS):
         fr = fres[...]
-        p = res[...] - product3(fr, aghi[...], aglo[...])
+        p = res[...] - product3(fr, aghi[:, :2048], aglo[:, :2048])
         w = kres[...] - product3(fr, kaghi[...], kaglo[...])
         put_blocks(w)
         part = block_sum(w, p)
-        swap(2 * it)
+        going = swap(2 * it)
+        spread_out(1 + 2 * it, payload(w, part))
+        for copy in going:
+            copy.wait_recv()
         for b in range(16):
             zvec[:, b * 128 : b * 128 + 128] = assembled(2 * it, b)
-        spread_out(1 + 2 * it, payload(zvec[...], part))
         for s in range(2):
             def store(cols, value):
                 szvec[:, cols] = value
 
             apply(shi, slo, s, zvec[:, s * 1024 : s * 1024 + 1024], store)
         fz, rho = factors(1 + 2 * it)
-        y = zvec[...] - product3(fz, aghi[...], aglo[...])
+        y = zvec[...] - product3(fz, aghi[:, :2048], aglo[:, :2048])
         q = szvec[...] - product3(fz, saghi[...], saglo[...])
         if it > 0:
             beta = rho / rho_before
@@ -374,10 +410,12 @@
         qvec[...] = q
         put_blocks(q)
         part = block_sum(q, y)
-        swap(2 * it + 1)
+        going = swap(2 * it + 1)
+        spread_out(2 + 2 * it, payload(q, part))
+        for copy in going:
+            copy.wait_recv()
         for b in range(16):
             zvec[:, b * 128 : b * 128 + 128] = assembled(2 * it + 1, b)
-        spread_out(2 + 2 * it, payload(zvec[...], part))
         if it + 1 < ITERS:
             for s in range(2):
                 def store(cols, value):
@@ -399,16 +437,19 @@
         fres[...] = fres[...] - step * fi
         rho_before = rho
 
-    p = res[...] - product3(fres[...], aghi[...], aglo[...])
+    p = res[...] - product3(fres[...], aghi[:, :2048], aglo[:, :2048])
     for s in range(2):
         out_ref[s] = p[:, s * 1024 : s * 1024 + 1024]
 
-    for _, copy in first:
-        copy.wait_send()
-    for copy in swaps:
+    for copy in first[0] + first[1] + first[2] + [hand] + swaps + mates:
         copy.wait_send()
     for k in range(GATHERS):
         wait_all(ssemg, k)
+
+
+def hand_over(a_ref, b_ref, c_ref, d_ref):
+    c_ref[...] = a_ref[...]
+    d_ref[...] = b_ref[...]
 
 
 def per_device(f_local, schur, precond, modes, coarse_inv, nbr_sub, nbr_blk):
@@ -416,16 +457,18 @@
     vec = pltpu.VMEM((16, 2048), F32)
     out = jax.ShapeDtypeStruct((2, 16, 1024), F32)
     anywhere = pl.BlockSpec(memory_space=pl.ANY)
+    inside = pl.BlockSpec(memory_space=pltpu.VMEM)
     smem = pl.BlockSpec(memory_space=pltpu.SMEM)
     half = pltpu.VMEM((2, 1024, 1024), BF16)
     tall = pltpu.VMEM((ROWS, 2048), BF16)
+    wide = pltpu.VMEM((ROWS, 2176), BF16)
     blocks = pltpu.VMEM((17, 16, 128), F32)
     table = pltpu.SMEM((16,), jnp.int32)
-    return pl.pallas_call(
+    found = pl.pallas_call(
         kernel,
         out_shape=(out, out),
         in_specs=[smem, smem] + [anywhere] * 5,
-        out_specs=(pl.BlockSpec(memory_space=pltpu.VMEM),) * 2,
+        out_specs=(inside,) * 2,
         scratch_shapes=[
             pltpu.VMEM((2, 16, 1024), F32), pltpu.VMEM((6, 2, 1024), F32),
             pltpu.VMEM((12, 1536), F32), pltpu.VMEM((16, 1536), F32), pltpu.VMEM((768, 768), BF16),
@@ -434,21 +477,27 @@
             pltpu.VMEM((16, 16, 128), F32), pltpu.VMEM((17, 16, 128), F32),
             pltpu.VMEM((16, 8, 128), F32), pltpu.VMEM((16, 8, 128), F32), pltpu.VMEM((16, 8, 128), F32),
             pltpu.VMEM((128, 1536), F32), pltpu.VMEM((1536, 256), BF16),
-            tall, tall, tall, tall, tall, tall,
-            pltpu.VMEM((16, 2176), BF16), pltpu.VMEM((16, 2176), BF16),
+            wide, wide, tall, tall, tall, tall,
             pltpu.VMEM((SWAPS, 16, 16, 128), F32), blocks, blocks, blocks, blocks,
             pltpu.VMEM((16, 16, 128), F32),
-            pltpu.VMEM((GATHERS, 128, 2, 128), F32),
+            pltpu.VMEM((GATHERS, 5, 64, 2, 128), F32),
+            pltpu.VMEM((GATHERS, 16, 128), F32), pltpu.VMEM((GATHERS, 16, 128), F32),
             vec, vec, vec, vec, vec, vec,
             pltpu.VMEM((16, ROWS), F32),
-            dma((7,)), dma((12,)), dma((12,)), dma((SWAPS, 4)), dma((SWAPS, 4)),
-            dma((GATHERS,)), dma((GATHERS,)),
+            dma((7,)), dma((13,)), dma((13,)), dma((SWAPS, 4)), dma((SWAPS, 4)),
+            dma((GATHERS,)), dma((GATHERS,)), dma((GATHERS,)), dma((GATHERS,)),
         ],
         compiler_params=pltpu.CompilerParams(
             collective_id=0, has_side_effects=True, vmem_limit_bytes=56 * 2**20
         ),
         cost_estimate=pl.CostEstimate(flops=10**9, bytes_accessed=2 * 10**7, transcendentals=0),
     )(nbr_sub, nbr_blk, f_local, schur, precond, modes.transpose(1, 0, 2), coarse_inv)
+    return pl.pallas_call(
+        hand_over,
+        out_shape=(out, out),
+        in_specs=[inside] * 2,
+        out_specs=(inside,) * 2,
+    )(*found)
 
 
 def solution(mesh):

time: 77.1 us -> 68.7 us (0.89)
  Pallas kernels: 73.2 us -> 68 us
  local copies, waits for them, and re-layouts: 3.14 us -> 0 us
    pallas_call x1, Pallas kernels: 73.2 us -> 66.3 us  [per_device(): pl.pallas_call(kernel, out_shape=(out, out), in_specs=[smem, smem] + [any...]
    unnamed x2 -> x0, local copies, waits for them, and re-layouts: 3.14 us -> none
    pallas_call x0 -> x1, Pallas kernels: none -> 1.68 us  [per_device(): pl.pallas_call(hand_over, out_shape=(out, out), in_specs=[inside] * 2, ou...]
where the time goes in v3:
time: 68.7 us; the launch traced here: 68.6 us
  Pallas kernels  68 us (99%)
    pallas_call x1, Pallas kernels, per_device(): pl.pallas_call(kernel, out_shape=(out, out), in_specs=[smem, smem] + [any...  66.3 us
    pallas_call x1, Pallas kernels, per_device(): pl.pallas_call(hand_over, out_shape=(out, out), in_specs=[inside] * 2, ou...  1.68 us

profile of v3, /device:TPU:1, one launch (start us, length us, event | category | flops | bytes accessed | tf_op | source)
XLA Modules:
  0.0 68.6 jit_solution(9687160305453731626)
XLA Ops:
  0.6 66.3 %shard_map.86 = (f32[2,16,1024]{2,1,0:T(8,128)}, f32[2,16,1024]{2,1,0:T(8,128)}) custom-call(s32[2,8]{1,0:T(2,128)} %nsub_ref.1, s32[2,8]{1,0:T(2,128)} %nblk_ref.1, f32[2,16,1024]{2,1,0:T(8,128)} %f_hbm.1, f32[2,1024,1024]{2,1,0:T(8,128)} %schur_hbm.1, f32[2,1024,1024]{2,1,0:T(8,128)} %precond_hbm.1, f32[6,2,1024]{2,1,0:T(2,128)} %bitcast.1, ...), custom_call_target="tpu_custom_call" | custom-call | flops 1000000000 | bytes 20000000 | tf_op jit(solution)/shard_map/pallas_call | solution.py:467
  66.9 1.7 %shard_map.87 = (f32[2,16,1024]{2,1,0:T(8,128)}, f32[2,16,1024]{2,1,0:T(8,128)}) custom-call(f32[2,16,1024]{2,1,0:T(8,128)} %get-tuple-element.4.a_ref, f32[2,16,1024]{2,1,0:T(8,128)} %get-tuple-element.5.b_ref), custom_call_target="tpu_custom_call" | custom-call | tf_op jit(solution)/shard_map/pallas_call | solution.py:495

commit v4 on v3

--- a/solution.py
+++ b/solution.py
@@ -43,7 +43,7 @@
     fsend, frecv, mown, msend, mrecv, crows, cboth,
     aghi, aglo, kaghi, kaglo, saghi, saglo,
     wsend, wrecv0, wrecv1, wrecv2, wrecv3, wblk, gath, fpart, fmate,
-    res, kres, zvec, szvec, dirv, qvec, fres,
+    res, kres, zvec, szvec, dirv, qvec, fres, tkhi, tklo, tshi, tslo,
     hsem, ssem0, rsem0, ssemx, rsemx, ssemg, rsemg, ssemf, rsemf,
 ):
     i, j = lax.axis_index("sub"), lax.axis_index("blk")
@@ -168,8 +168,9 @@
         both = dot(jnp.concatenate([ch, cl], axis=0), order[...])
         crows[0:16, cols] = both[:16] + both[16:]
     row = lax.broadcasted_iota(jnp.int32, (ROWS, 128), 0)
-    aghi[:, 2048:2176] = jnp.where(row == 6, 1.0, 0.0).astype(BF16)
-    aglo[:, 2048:2176] = jnp.zeros((ROWS, 128), BF16)
+    for n, at in enumerate((6, 7, 14)):
+        aghi[:, 2048 + 128 * n : 2176 + 128 * n] = jnp.where(row == at, 1.0, 0.0).astype(BF16)
+    aglo[:, 2048:2432] = jnp.zeros((ROWS, 384), BF16)
     for t in range(16):
         fsend[t] = wblk[pick[t]]
         msend[t] = mown[pick[t]]
@@ -230,15 +231,28 @@
     lane = lax.broadcasted_iota(jnp.int32, (ROWS, 128), 1)
     own = (lane // 16) == lax.rem(row, 8)
 
-    def payload(vec, scalar):
-        u = jnp.concatenate([vec, scalar], axis=1)
+    real = lax.rem(row, 8) < 6
+    nothing = jnp.zeros((16, 128), F32)
+
+    def onto(vec, sums):
+        sums = list(sums) + [nothing] * (3 - len(sums))
+        u = jnp.concatenate([vec] + sums, axis=1)
         uh, ul = split(u)
         uh = jnp.concatenate([uh] * 8, axis=0)
         ul = jnp.concatenate([ul] * 8, axis=0)
         both = dot_t(jnp.concatenate([aghi[...], aglo[...]], axis=0), uh)
-        r = both[:ROWS] + both[ROWS:] + dot_t(aghi[...], ul)
-        r = jnp.where(own, r, 0.0)
-        return jnp.sum(r.reshape(5, 2, 8, 128), axis=2)
+        return both[:ROWS] + both[ROWS:] + dot_t(aghi[...], ul)
+
+    def pack(r):
+        return jnp.sum(jnp.where(own, r, 0.0).reshape(5, 2, 8, 128), axis=2)
+
+    def times(hi, lo, x):
+        xh, xl = split(x)
+        both = dot(jnp.concatenate([hi[...], lo[...]], axis=0), xh)
+        return both[:ROWS] + both[ROWS:] + dot(hi[...], xl)
+
+    def fold(x):
+        return jnp.sum(x, axis=0, keepdims=True)
 
     def spread_out(k, value):
         mine = gath.at[k, :, slot]
@@ -255,7 +269,7 @@
 
     mates = []
 
-    def factors(k):
+    def factors(k, beside):
         wait_all(rsemg, k)
         mine, plus, minus, along, mate = [gath.at[k, n].reshape(128, 128)[...] for n in range(5)]
         same = mine + jnp.concatenate([plus[120:], plus[:120]], axis=0)
@@ -289,10 +303,15 @@
         )
         copy.start()
         mates.append(copy)
+        more = beside()
         copy.wait_recv()
         mates_part = fmate[k]
         total = part + pltpu.roll(mates_part, 64, 1)
-        return total[:, :ROWS], part[:, 6:7] + mates_part[:, 6:7]
+        turned = jnp.concatenate([total] * 8, axis=0).T
+        return (
+            total[:, :ROWS], part[:, 6:7] + mates_part[:, 6:7],
+            jnp.where(real, turned[:ROWS], 0.0), turned[6:7] + turned[70:71], more,
+        )
 
     def apply(hi_ref, lo_ref, s, vec, store):
         for q in range(4):
@@ -333,7 +352,7 @@
         for b in range(16):
             wblk[b] = x[:, b * 128 : b * 128 + 128]
 
-    spread_out(0, payload(jnp.concatenate([wblk[b] for b in range(16)], axis=1), jnp.zeros((16, 128), F32)))
+    spread_out(0, pack(onto(jnp.concatenate([wblk[b] for b in range(16)], axis=1), [])))
     for copy in first[1]:
         copy.wait_recv()
     for b in range(16):
@@ -379,51 +398,35 @@
     cboth[:, 0:128] = h
     cboth[:, 128:256] = l
 
-    fr, _ = factors(0)
-    fres[...] = fr
-    rho_before = None
-    for it in range(ITERS):
-        fr = fres[...]
-        p = res[...] - product3(fr, aghi[:, :2048], aglo[:, :2048])
-        w = kres[...] - product3(fr, kaghi[...], kaglo[...])
-        put_blocks(w)
-        part = block_sum(w, p)
-        going = swap(2 * it)
-        spread_out(1 + 2 * it, payload(w, part))
+    def coupling(ahi, alo, out_hi, out_lo):
+        h, l = aghi[:, :2048], aglo[:, :2048]
+        both = dot_t(jnp.concatenate([h, l], axis=0), ahi[...])
+        out_hi[...], out_lo[...] = split(both[:ROWS] + both[ROWS:] + dot_t(h, alo[...]))
+
+    def at_start():
+        coupling(kaghi, kaglo, tkhi, tklo)
+        coupling(saghi, saglo, tshi, tslo)
+        return onto(kres[...], [block_sum(kres[...], res[...])])
+
+    def collect(k, going):
         for copy in going:
             copy.wait_recv()
         for b in range(16):
-            zvec[:, b * 128 : b * 128 + 128] = assembled(2 * it, b)
+            zvec[:, b * 128 : b * 128 + 128] = assembled(k, b)
+
+    def apply_all(hi_ref, lo_ref):
+        def store(cols, value):
+            szvec[:, cols] = value
+
         for s in range(2):
-            def store(cols, value):
-                szvec[:, cols] = value
-
-            apply(shi, slo, s, zvec[:, s * 1024 : s * 1024 + 1024], store)
-        fz, rho = factors(1 + 2 * it)
-        y = zvec[...] - product3(fz, aghi[:, :2048], aglo[:, :2048])
-        q = szvec[...] - product3(fz, saghi[...], saglo[...])
-        if it > 0:
-            beta = rho / rho_before
-            y = y + beta * dirv[...]
-            q = q + beta * qvec[...]
-        dirv[...] = y
-        qvec[...] = q
-        put_blocks(q)
-        part = block_sum(q, y)
-        going = swap(2 * it + 1)
-        spread_out(2 + 2 * it, payload(q, part))
-        for copy in going:
-            copy.wait_recv()
-        for b in range(16):
-            zvec[:, b * 128 : b * 128 + 128] = assembled(2 * it + 1, b)
-        if it + 1 < ITERS:
-            for s in range(2):
-                def store(cols, value):
-                    szvec[:, cols] = value
-
-                apply(khi, klo, s, zvec[:, s * 1024 : s * 1024 + 1024], store)
-        fi, sigma = factors(2 + 2 * it)
-        step = rho / sigma
+            apply(hi_ref, lo_ref, s, zvec[:, s * 1024 : s * 1024 + 1024], store)
+
+    fr, _, frep, _, g = factors(0, at_start)
+    fres[...] = fr
+    energy = g[6:7]
+    step = rho_row = None
+
+    def advance(it):
         for s in range(2):
             cols = slice(s * 1024, s * 1024 + 1024)
             add = step * dirv[:, cols]
@@ -434,9 +437,76 @@
         res[...] = res[...] - step * zvec[...]
         if it + 1 < ITERS:
             kres[...] = kres[...] - step * szvec[...]
+
+    for it in range(ITERS):
+        if it > 0:
+            advance(it - 1)
+        put_blocks(kres[...] - product3(fres[...], kaghi[...], kaglo[...]))
+        going = swap(2 * it)
+        u = g - times(tkhi, tklo, frep)
+        scalar = energy - fold(frep * (g + u))
+        u = jnp.where(real, u, 0.0)
+        spread_out(1 + 2 * it, pack(jnp.where(row == 6, scalar, u)))
+        collect(2 * it, going)
+        apply_all(shi, slo)
+
+        def beside():
+            sums = [block_sum(zvec[...], szvec[...])]
+            if it > 0:
+                sums.append(block_sum(zvec[...], qvec[...]))
+            return onto(szvec[...], sums)
+
+        rho_before = rho_row
+        if it > 0:
+            rho_col = rho
+        fz, rho, frz, rho_row, g2 = factors(1 + 2 * it, beside)
+        going = None
+
+        def exchange():
+            q = szvec[...] - product3(fz, saghi[...], saglo[...])
+            if it > 0:
+                q = q + (rho / rho_col) * qvec[...]
+            qvec[...] = q
+            put_blocks(q)
+            return swap(2 * it + 1)
+
+        if it + 1 < ITERS:
+            going = exchange()
+        u = g2 - times(tshi, tslo, frz)
+        scalar = g2[6:7] - fold(frz * (g2 + u))
+        u = jnp.where(real, u, 0.0)
+        if it > 0:
+            beta = rho_row / rho_before
+            scalar = scalar + 2 * beta * (g2[7:8] - fold(frz * uq)) + beta * beta * bend
+            u = u + beta * uq
+        uq, bend = u, scalar
+        spread_out(2 + 2 * it, pack(jnp.where(row == 6, scalar, u)))
+        if it + 1 == ITERS:
+            going = exchange()
+        y = zvec[...] - product3(fz, aghi[:, :2048], aglo[:, :2048])
+        if it > 0:
+            y = y + (rho / rho_col) * dirv[...]
+        dirv[...] = y
+        collect(2 * it + 1, going)
+        if it + 1 < ITERS:
+            apply_all(khi, klo)
+
+        def beside():
+            if it + 1 == ITERS:
+                return None
+            return onto(
+                szvec[...], [block_sum(szvec[...], res[...]), block_sum(szvec[...], zvec[...])]
+            )
+
+        fi, sigma, fri, sigma_row, g3 = factors(2 + 2 * it, beside)
+        step, step_row = rho / sigma, rho_row / sigma_row
         fres[...] = fres[...] - step * fi
-        rho_before = rho
-
+        if it + 1 < ITERS:
+            frep = frep - step_row * fri
+            energy = energy - 2 * step_row * g3[6:7] + step_row * step_row * g3[7:8]
+            g = g - step_row * g3
+
+    advance(ITERS - 1)
     p = res[...] - product3(fres[...], aghi[:, :2048], aglo[:, :2048])
     for s in range(2):
         out_ref[s] = p[:, s * 1024 : s * 1024 + 1024]
@@ -461,7 +531,8 @@
     smem = pl.BlockSpec(memory_space=pltpu.SMEM)
     half = pltpu.VMEM((2, 1024, 1024), BF16)
     tall = pltpu.VMEM((ROWS, 2048), BF16)
-    wide = pltpu.VMEM((ROWS, 2176), BF16)
+    wide = pltpu.VMEM((ROWS, 2432), BF16)
+    small = pltpu.VMEM((ROWS, ROWS), BF16)
     blocks = pltpu.VMEM((17, 16, 128), F32)
     table = pltpu.SMEM((16,), jnp.int32)
     found = pl.pallas_call(
@@ -483,7 +554,7 @@
             pltpu.VMEM((GATHERS, 5, 64, 2, 128), F32),
             pltpu.VMEM((GATHERS, 16, 128), F32), pltpu.VMEM((GATHERS, 16, 128), F32),
             vec, vec, vec, vec, vec, vec,
-            pltpu.VMEM((16, ROWS), F32),
+            pltpu.VMEM((16, ROWS), F32), small, small, small, small,
             dma((7,)), dma((13,)), dma((13,)), dma((SWAPS, 4)), dma((SWAPS, 4)),
             dma((GATHERS,)), dma((GATHERS,)), dma((GATHERS,)), dma((GATHERS,)),
         ],

time: 68.7 us -> 67.9 us (0.988)
  Pallas kernels: 68 us -> 67.1 us
    pallas_call x1, Pallas kernels: 66.3 us -> 65.4 us  [per_device(): pl.pallas_call(kernel, out_shape=(out, out), in_specs=[smem, smem] + [any...]
where the time goes in v4:
time: 67.9 us; the launch traced here: 67.7 us
  Pallas kernels  67.1 us (99%)
    pallas_call x1, Pallas kernels, per_device(): pl.pallas_call(kernel, out_shape=(out, out), in_specs=[smem, smem] + [any...  65.4 us
    pallas_call x1, Pallas kernels, per_device(): pl.pallas_call(hand_over, out_shape=(out, out), in_specs=[inside] * 2, ou...  1.68 us

profile of v4, /device:TPU:1, one launch (start us, length us, event | category | flops | bytes accessed | tf_op | source)
XLA Modules:
  0.0 67.7 jit_solution(18003511544441248882)
XLA Ops:
  0.6 65.4 %shard_map.86 = (f32[2,16,1024]{2,1,0:T(8,128)}, f32[2,16,1024]{2,1,0:T(8,128)}) custom-call(s32[2,8]{1,0:T(2,128)} %nsub_ref.1, s32[2,8]{1,0:T(2,128)} %nblk_ref.1, f32[2,16,1024]{2,1,0:T(8,128)} %f_hbm.1, f32[2,1024,1024]{2,1,0:T(8,128)} %schur_hbm.1, f32[2,1024,1024]{2,1,0:T(8,128)} %precond_hbm.1, f32[6,2,1024]{2,1,0:T(2,128)} %bitcast.1, ...), custom_call_target="tpu_custom_call" | custom-call | flops 1000000000 | bytes 20000000 | tf_op jit(solution)/shard_map/pallas_call | solution.py:538
  66.0 1.7 %shard_map.87 = (f32[2,16,1024]{2,1,0:T(8,128)}, f32[2,16,1024]{2,1,0:T(8,128)}) custom-call(f32[2,16,1024]{2,1,0:T(8,128)} %get-tuple-element.4.a_ref, f32[2,16,1024]{2,1,0:T(8,128)} %get-tuple-element.5.b_ref), custom_call_target="tpu_custom_call" | custom-call | tf_op jit(solution)/shard_map/pallas_call | solution.py:566

commit v5 on v3

--- a/solution.py
+++ b/solution.py
@@ -410,8 +410,11 @@
         qvec[...] = q
         put_blocks(q)
         part = block_sum(q, y)
-        going = swap(2 * it + 1)
+        if it + 1 < ITERS:
+            going = swap(2 * it + 1)
         spread_out(2 + 2 * it, payload(q, part))
+        if it + 1 == ITERS:
+            going = swap(2 * it + 1)
         for copy in going:
             copy.wait_recv()
         for b in range(16):

time: 68.7 us -> 68.5 us (level)
  no operation moved by 1% of the time
where the time goes in v5:
time: 68.5 us; the launch traced here: 68.3 us
  Pallas kernels  67.7 us (99%)
    pallas_call x1, Pallas kernels, per_device(): pl.pallas_call(kernel, out_shape=(out, out), in_specs=[smem, smem] + [any...  66 us
    pallas_call x1, Pallas kernels, per_device(): pl.pallas_call(hand_over, out_shape=(out, out), in_specs=[inside] * 2, ou...  1.68 us

profile of v5, /device:TPU:1, one launch (start us, length us, event | category | flops | bytes accessed | tf_op | source)
XLA Modules:
  0.0 68.3 jit_solution(3606567394609679913)
XLA Ops:
  0.6 66.0 %shard_map.86 = (f32[2,16,1024]{2,1,0:T(8,128)}, f32[2,16,1024]{2,1,0:T(8,128)}) custom-call(s32[2,8]{1,0:T(2,128)} %nsub_ref.1, s32[2,8]{1,0:T(2,128)} %nblk_ref.1, f32[2,16,1024]{2,1,0:T(8,128)} %f_hbm.1, f32[2,1024,1024]{2,1,0:T(8,128)} %schur_hbm.1, f32[2,1024,1024]{2,1,0:T(8,128)} %precond_hbm.1, f32[6,2,1024]{2,1,0:T(2,128)} %bitcast.1, ...), custom_call_target="tpu_custom_call" | custom-call | flops 1000000000 | bytes 20000000 | tf_op jit(solution)/shard_map/pallas_call | solution.py:470
  66.7 1.7 %shard_map.87 = (f32[2,16,1024]{2,1,0:T(8,128)}, f32[2,16,1024]{2,1,0:T(8,128)}) custom-call(f32[2,16,1024]{2,1,0:T(8,128)} %get-tuple-element.4.a_ref, f32[2,16,1024]{2,1,0:T(8,128)} %get-tuple-element.5.b_ref), custom_call_target="tpu_custom_call" | custom-call | tf_op jit(solution)/shard_map/pallas_call | solution.py:498
